TPU v7x, 256 devices: a whole 4x4x8 slice. The times are simulated.
256 devices in a mesh: ctx: 32 (over z, x), exp: 8 (over y, core).
Axes of the slice: x: 4, y: 4, z: 8, core: 2. Of those that a mesh axis runs over, the one named last changes fastest.
Arguments:
- queries: bfloat16 [16, 2, 128, 576], P('exp'), may hold values from -300 to 300
- new_latent: bfloat16 [16, 2, 576], P('exp'), may hold values from -8 to 8
- cache: bfloat16 [16, 16384, 576], P('exp', 'ctx'), may hold values from -6 to 6
- lengths: int32 [16], P('exp'), may hold values from 4096 to 16384, as said below
- value_up: bfloat16 [128, 512, 128], P('ctx'), may hold values from -1 to 1
- out_proj: bfloat16 [16384, 7168], P(('ctx', 'exp')), may hold values from -0.046875 to 0.046875
- residual: bfloat16 [16, 2, 7168], P('exp', None, 'ctx'), may hold values from -9 to 9
- norm_gain: float32 [7168], P('ctx'), may hold values from 0.1 to 1.9
- route_ids: int32 [16, 2, 8], P('exp'), may hold values from 0 to 15, all different within a row; in each aligned block of 4 rows (0 to 3, 4 to 7, ..., all dimensions but the last counted through in order) at most 4 rows name the same one
- route_weights: float32 [16, 2, 8], P('exp'), may hold values from 0.05 to 0.5
- gate_up: bfloat16 [16, 7168, 4096], P('exp', 'ctx'), may hold values from -0.0625 to 0.0625
- expert_down: bfloat16 [16, 2048, 7168], P('exp', None, 'ctx'), may hold values from -0.125 to 0.125
Outputs:
- mixed: bfloat16 [16, 2, 7168], P('exp', None, 'ctx')
Inputs may be any that keep to these rules, and one draw needn't show every extreme that they name: `lengths`: some sequence has all 16384 positions cached. `route_ids`: each token names 8 different experts; on the tokens of one index of exp some expert is named by all 4 of them.
All inputs are finite; a program needn't handle non-finite values.
Results may differ from a plain program's by a relative error of at most 0.025.
Values may be sent and summed in bfloat16 or wider, within the bound.
A program may use at most 128 MiB of HBM per device.

v0:
```python
import math

import jax
import jax.numpy as jnp
from jax import lax
from jax.sharding import PartitionSpec as P

D = 7168
HEADS = 128
LATENT = 512
ROPE = 64
FFE = 2048
TOPK = 8
STEPS = 2


qk_scale = 1.0 / math.sqrt(192.0)
norm_eps = 1e-06


def combined_all(part, axis, combine):
    gathered = jax.tree.map(lambda a: lax.all_gather(a, axis), part)

    def take(source):
        return jax.tree.map(lambda a: lax.dynamic_index_in_dim(a, source, 0, False), gathered)

    return lax.fori_loop(
        1, lax.axis_size(axis), lambda source, state: combine(state, take(source)), take(0)
    )


def softmax_parts(query_rows, key_rows, visible):
    scores = (
        jnp.einsum("rqd,rkd->rqk", query_rows, key_rows, preferred_element_type=jnp.float32)
        * qk_scale
    )
    scores = jnp.where(visible, scores, -1e30)
    peak_score = jnp.max(scores, axis=2)
    weights = jnp.where(visible, jnp.exp(scores - peak_score[..., None]), 0.0)
    denom = jnp.sum(weights, axis=2)
    mixture = jnp.einsum(
        "rqk,rkl->rql",
        weights.astype(jnp.bfloat16),
        key_rows[..., :LATENT],
        preferred_element_type=jnp.float32,
    )
    return (mixture, peak_score, denom)


def join_parts(left_part, right_part):
    peak_score = jnp.maximum(left_part[1], right_part[1])
    left_scale = jnp.exp(left_part[1] - peak_score)
    right_scale = jnp.exp(right_part[1] - peak_score)
    mixture = left_part[0] * left_scale[..., None] + right_part[0] * right_scale[..., None]
    denom = left_part[2] * left_scale + right_part[2] * right_scale
    return (mixture, peak_score, denom)


def on_device(
    queries,
    new_latent,
    cache,
    lengths,
    value_up,
    out_proj,
    residual,
    norm_gain,
    route_ids,
    route_weights,
    gate_up,
    expert_down,
):
    row_count = queries.shape[0]
    ctx_span = cache.shape[1]
    tok_count = row_count * STEPS
    ctx_index = lax.axis_index("ctx")
    n_exp = lax.axis_size("exp")
    query_rows = queries.reshape(row_count, STEPS * HEADS, LATENT + ROPE)
    position = ctx_index * ctx_span + jnp.arange(ctx_span, dtype=jnp.int32)
    visible = jnp.broadcast_to(
        (position[None, :] < lengths[:, None])[:, None, :], (row_count, STEPS * HEADS, ctx_span)
    )
    step_of = jnp.arange(STEPS * HEADS, dtype=jnp.int32) // HEADS
    causal = (jnp.arange(STEPS, dtype=jnp.int32)[None, :] <= step_of[:, None]) & (ctx_index == 0)
    fresh_visible = jnp.broadcast_to(causal[None], (row_count, STEPS * HEADS, STEPS))
    pieces = join_parts(
        softmax_parts(query_rows, cache, visible),
        softmax_parts(query_rows, new_latent, fresh_visible),
    )
    mixture = pieces[0].reshape(tok_count, HEADS, LATENT)
    peak_score = pieces[1].reshape(tok_count, HEADS)
    denom = pieces[2].reshape(tok_count, HEADS)
    local_heads = value_up.shape[0]
    mixture, peak_score, denom = combined_all((mixture, peak_score, denom), "ctx", join_parts)
    offset = ctx_index * local_heads
    mixture = lax.dynamic_slice_in_dim(mixture, offset, local_heads, 1)
    denom = lax.dynamic_slice_in_dim(denom, offset, local_heads, 1)
    latent_out = mixture / denom[..., None]
    values = jnp.einsum(
        "thl,hlv->thv", latent_out, value_up.astype(jnp.float32), precision=lax.Precision.HIGHEST
    ).astype(jnp.bfloat16)
    values = values.reshape(tok_count, n_exp, -1)
    spread = lax.all_to_all(values, "exp", split_axis=1, concat_axis=0, tiled=True).reshape(
        n_exp * tok_count, -1
    )
    attn_rows = lax.psum_scatter(
        jnp.dot(spread, out_proj, preferred_element_type=jnp.float32),
        "exp",
        scatter_dimension=0,
        tiled=True,
    )
    attn_out = lax.psum_scatter(attn_rows, "ctx", scatter_dimension=1, tiled=True)
    hidden = (residual.reshape(tok_count, -1).astype(jnp.float32) + attn_out).astype(jnp.bfloat16)
    hidden_f = hidden.astype(jnp.float32)
    squares = lax.psum(jnp.sum(hidden_f * hidden_f, axis=1), "ctx")
    normed = (hidden_f * lax.rsqrt(squares / D + norm_eps)[:, None] * norm_gain[None, :]).astype(
        jnp.bfloat16
    )
    exp_dev = gate_up.shape[0]
    route_list = route_ids.reshape(tok_count, TOPK)
    route_coef = route_weights.reshape(tok_count, TOPK)
    expert_grid = jnp.arange(n_exp * exp_dev, dtype=jnp.int32).reshape(n_exp, exp_dev)
    matches = route_list[:, :, None, None] == expert_grid[None, None, :, :]
    chosen = jnp.any(matches, axis=1)
    mix_coef = jnp.sum(route_coef[:, :, None, None] * matches.astype(jnp.float32), axis=1)
    outgoing = jnp.where(
        jnp.transpose(chosen, (2, 1, 0))[..., None], normed[None, None], jnp.zeros((), jnp.bfloat16)
    )
    incoming = lax.all_to_all(outgoing, "exp", split_axis=1, concat_axis=1, tiled=True).reshape(
        exp_dev, n_exp * tok_count, -1
    )
    gate_up_sum = jnp.einsum("jnd,jdf->jnf", incoming, gate_up, preferred_element_type=jnp.float32)
    gate_up_sum = lax.psum(gate_up_sum, "ctx")
    activated = (jax.nn.silu(gate_up_sum[..., :FFE]) * gate_up_sum[..., FFE:]).astype(jnp.bfloat16)
    expert_out = jnp.einsum(
        "jnf,jfd->jnd", activated, expert_down, preferred_element_type=jnp.float32
    )
    expert_out = expert_out.astype(jnp.bfloat16).reshape(exp_dev, n_exp, tok_count, -1)
    returned = lax.all_to_all(expert_out, "exp", split_axis=1, concat_axis=1, tiled=True)
    routed = jnp.einsum(
        "toj,jotd->td", mix_coef, returned.astype(jnp.float32), precision=lax.Precision.HIGHEST
    )
    mixed = (hidden_f + routed).astype(jnp.bfloat16)
    return mixed.reshape(row_count, STEPS, -1)


def solution(mesh):
    in_specs = (
        P("exp", None, None, None),
        P("exp", None, None),
        P("exp", "ctx", None),
        P("exp"),
        P("ctx", None, None),
        P(("ctx", "exp"), None),
        P("exp", None, "ctx"),
        P("ctx"),
        P("exp", None, None),
        P("exp", None, None),
        P("exp", "ctx", None),
        P("exp", None, "ctx"),
    )
    out_specs = P("exp", None, "ctx")
    return jax.shard_map(
        on_device, mesh=mesh, in_specs=in_specs, out_specs=out_specs, check_vma=False
    )
```

profile of v0, /device:TPU:1, one launch (start us, length us, event | category | flops | bytes accessed | tf_op | source)
XLA Modules:
  0.0 851.5 jit_solution(17642897557874663256)
XLA Ops:
  6.6 0.9 broadcast_compare_fusion
  7.5 2.2 fusion.38
  9.8 0.2 fusion.37
  10.0 0.5 convolution_multiply_fusion.1
  10.5 1.3 fusion.3
  12.0 0.3 fusion.8
  12.4 43.9 %all_gather.11 = f32[32,4,128]{2,1,0:T(4,128)S(1)} all-gather(f32[1,4,128]{2,1,0:T(4,128)S(1)} %get-tuple-element.204), channel_id=1, replica_groups=mesh['ctx'=32,'exp'=8] {'ctx'}, dimensions={0}, use_global_device_ids=true | all-gather | bytes 67584 | tf_op jit(solution)/shard_map/all_gather | solution.py:22
  56.3 38.4 %all_gather.10 = f32[32,4,128]{2,1,0:T(4,128)S(1)} all-gather(f32[1,4,128]{2,1,0:T(4,128)S(1)} %get-tuple-element.205), channel_id=1, replica_groups=mesh['ctx'=32,'exp'=8] {'ctx'}, dimensions={0}, use_global_device_ids=true | all-gather | bytes 67584 | tf_op jit(solution)/shard_map/all_gather | solution.py:22
  94.7 154.7 %all-gather.2.cloned.1.call-done = f32[32,4,128,512]{3,2,1,0:T(8,128)} async-done(((f32[1,4,128,512]{3,2,1,0:T(8,128)}), f32[32,4,128,512]{3,2,1,0:T(8,128)}) %all-gather.2.cloned.1.call-update) | async-done | bytes 33554448 | tf_op jit(solution)/shard_map/all_gather | solution.py:22
  249.4 1.3 slice_bitcast_fusion
  250.7 49.2 %while.19 = (s32[]{:T(128)}, f32[4,128,512]{2,1,0:T(8,128)S(1)}, f32[4,128]{1,0:T(4,128)S(1)}, f32[4,128]{1,0:T(4,128)S(1)}, f32[32,4,128]{2,1,0:T(4,128)S(1)}, ...) while((s32[]{:T(128)}, f32[4,128,512]{2,1,0:T(8,128)S(1)}, ...), condition=%wide.region_5.6_spmd, body=%wide.region_4.5_spmd.sunk | while | flops 789509 | bytes 3166359 | solution.py:27
  250.7 1.6 fusion.55
  252.3 1.5 fusion.55
  253.9 1.5 fusion.55
  255.5 1.5 fusion.55
  257.1 1.5 fusion.55
  258.7 1.5 fusion.55
  260.3 1.5 fusion.55
  261.9 1.5 fusion.55
  263.4 1.5 fusion.55
  265.0 1.5 fusion.55
  266.6 1.5 fusion.55
  268.2 1.5 fusion.55
  269.8 1.5 fusion.55
  271.4 1.5 fusion.55
  273.0 1.5 fusion.55
  274.5 1.5 fusion.55
  276.1 1.5 fusion.55
  277.7 1.5 fusion.55
  279.3 1.5 fusion.55
  280.9 1.5 fusion.55
  282.5 1.5 fusion.55
  284.1 1.5 fusion.55
  285.6 1.5 fusion.55
  287.2 1.5 fusion.55
  288.8 1.5 fusion.55
  290.4 1.5 fusion.55
  292.0 1.5 fusion.55
  293.6 1.5 fusion.55
  295.1 1.5 fusion.55
  296.7 1.5 fusion.55
  298.3 1.5 fusion.55
  300.0 0.3 fusion.6
  300.6 9.6 %all_to_all.25 = bf16[8,2,128]{2,1,0:T(2,128)(2,1)S(1)} all-to-all(bf16[8,2,128]{2,1,0:T(2,128)(2,1)S(1)} %reshape.200), channel_id=1, replica_groups=mesh['ctx'=32,'exp'=8] {'exp'}, dimensions={0} | all-to-all | bytes 8192 | tf_op jit(solution)/shard_map/all_to_all | solution.py:103
  310.3 2.4 fusion.39
  312.8 0.6 dynamic-slice
  314.0 59.1 %all-reduce.6.cloned.1.call-done = f32[32,7168]{1,0:T(8,128)} async-done(((f32[32,7168]{1,0:T(8,128)}), f32[32,7168]{1,0:T(8,128)}) %all-reduce.6.cloned.1.call-update) | async-done | bytes 917520
  373.2 1.0 constant_dynamic-slice_fusion
  374.1 2.4 copy.38
  376.6 0.6 copy-done.4
  377.4 0.1 copy.32
  377.5 217.1 %reduce-scatter.4.cloned.1.call-done = f32[224,4]{1,0:T(8,128)} async-done(((f32[7168,4]{1,0:T(8,128)}), f32[224,4]{1,0:T(8,128)}) %reduce-scatter.4.cloned.1.call-update) | async-done | bytes 3600
  594.6 1.0 copy.39
  595.5 0.1 fusion.25
  595.7 58.8 %psum.14 = f32[4]{0:T(128)S(1)} all-reduce(f32[4]{0:T(128)S(1)} %get-tuple-element.202), channel_id=1, replica_groups=mesh['ctx'=32,'exp'=8] {'ctx'}, use_global_device_ids=true, to_apply=%region_11.12 | all-reduce | flops 4 | bytes 32 | tf_op jit(solution)/shard_map/psum | solution.py:115
  654.7 27.9 %all_to_all.26 = bf16[2,8,4,224]{3,2,0,1:T(4,128)(2,1)S(1)} all-to-all(bf16[2,8,4,224]{3,2,0,1:T(4,128)(2,1)S(1)} %broadcast_select_fusion), channel_id=1, replica_groups=mesh['ctx'=32,'exp'=8] {'exp'}, dimensions={1} | all-to-all | bytes 57344 | tf_op jit(solution)/shard_map/all_to_all | solution.py:129
  682.7 3.8 fusion.40
  686.6 140.8 %all-reduce.4.cloned.1.call-done = f32[2,32,4096]{2,1,0:T(8,128)} async-done(((f32[2,32,4096]{2,1,0:T(8,128)}), f32[2,32,4096]{2,1,0:T(8,128)}) %all-reduce.4.cloned.1.call-update) | async-done | bytes 1048592 | tf_op jit(solution)/shard_map/psum | solution.py:133
  827.3 1.9 convolution_convert_fusion
  829.2 0.6 copy.34
  829.8 9.6 %all-to-all-start.2 = ((bf16[2,8,4,224]{3,2,0,1:T(4,128)(2,1)}), bf16[2,8,4,224]{3,2,0,1:T(4,128)(2,1)S(1)}, u32[]{:S(2)}, u32[]{:S(2)}) async-start(bf16[2,8,4,224]{3,2,0,1:T(4,128)(2,1)} %copy.34), calls=%async_computation.2 | async-start | bytes 65536 | tf_op jit(solution)/shard_map/all_to_all | solution.py:139
  839.5 4.6 all-to-all-done.2
  844.1 0.2 fusion.22
  844.3 0.6 reshape.193
  (88 shorter events, 2.0 us)
Async XLA Ops:
  6.5 820.8 %copy-start = (bf16[2,2048,224]{1,2,0:T(8,128)(2,1)S(1)}, bf16[2,2048,224]{1,2,0:T(8,128)(2,1)}, u32[]{:S(2)}) copy-start(bf16[2,2048,224]{1,2,0:T(8,128)(2,1)} %param.25) | copy-start | bytes 5505028
  6.5 3.2 copy-start.8
  6.5 3.2 copy-start.3
  6.5 242.8 %all-gather.2.cloned.1.call-start = ((), (), s32[]{:S(2)}) async-start(), calls=%async_computation.4 | async-start | bytes 34603008 | tf_op jit(solution)/shard_map/all_gather | solution.py:22
  7.5 2.5 copy-start.7
  11.9 361.3 %all-reduce.6.cloned.1.call-start = ((), (), s32[]{:S(2)}) async-start(), calls=%async_computation.7 | async-start | bytes 1835008
  250.7 49.4 %copy-start.1 = (bf16[4,512,128]{2,1,0:T(8,128)(2,1)S(1)}, bf16[4,512,128]{2,1,0:T(8,128)(2,1)}, u32[]{:S(2)}) copy-start(bf16[4,512,128]{2,1,0:T(8,128)(2,1)} %param.18) | copy-start | bytes 1572868
  299.9 12.9 %copy-start.9 = (u32[256]{0:T(256)S(1)}, u32[256]{0:T(256)}, u32[]{:S(2)}) copy-start(u32[256]{0:T(256)} %constant.118) | copy-start | bytes 3076
  312.7 281.9 %reduce-scatter.4.cloned.1.call-start = ((), (), s32[]{:S(2)}) async-start(), calls=%async_computation.6 | async-start | bytes 3784704
  376.6 0.7 copy-start.4
  376.6 0.7 copy-start.2
  376.6 278.0 %copy-start.6 = (f32[224]{0:T(256)S(1)}, f32[224]{0:T(256)}, u32[]{:S(2)}) copy-start(f32[224]{0:T(256)} %param.21) | copy-start | bytes 2692
  376.6 450.8 %all-reduce.4.cloned.1.call-start = ((), (), s32[]{:S(2)}) async-start(), calls=%async_computation.5 | async-start | bytes 2097152 | tf_op jit(solution)/shard_map/psum | solution.py:133
  686.6 152.9 %copy-start.5 = (f32[2,2,8]{2,1,0:T(2,128)S(1)}, f32[2,2,8]{2,1,0:T(2,128)}, u32[]{:S(2)}) copy-start(f32[2,2,8]{2,1,0:T(2,128)} %param.23) | copy-start | bytes 388
  829.8 14.3 %all-to-all-start.2 = ((bf16[2,8,4,224]{3,2,0,1:T(4,128)(2,1)}), bf16[2,8,4,224]{3,2,0,1:T(4,128)(2,1)S(1)}, u32[]{:S(2)}, u32[]{:S(2)}) async-start(bf16[2,8,4,224]{3,2,0,1:T(4,128)(2,1)} %copy.34), calls=%async_computation.2 | async-start | bytes 65536 | tf_op jit(solution)/shard_map/all_to_all | solution.py:139
Sparse Core Ops, SparseCore 0:
  12.0 237.2 all-gather.1
  312.8 60.2 all-reduce.5
  377.6 216.9 reduce-scatter.3
  686.7 140.6 all-reduce.3
where the time goes:
time: 853 us; the launch traced here: 851 us
  waiting for transfers between devices  576 us (68%)
  blocking collectives  179 us (21%)
  other arithmetic  50.2 us (6%)
  between operations  14 us (2%)
  matrix products  13 us (2%)
  starting transfers between devices  9.68 us (1%)
  local copies, waits for them, and re-layouts  8.7 us (1%)
    unnamed x6, waiting for transfers between devices  276 us
    all_gather x1, waiting for transfers between devices, combined_all(): gathered = jax.tree.map(lambda a: lax.all_gather(a, axis), part)  155 us
    psum x1, waiting for transfers between devices, on_device(): gate_up_sum = lax.psum(gate_up_sum, 'ctx')  141 us
    all_gather x2, blocking collectives, combined_all(): gathered = jax.tree.map(lambda a: lax.all_gather(a, axis), part)  82.3 us
    psum x1, blocking collectives, on_device(): squares = lax.psum(jnp.sum(hidden_f * hidden_f, axis=1), 'ctx')  58.8 us
    add x31, other arithmetic, join_parts(): left_part[0] * left_scale[..., None]  47.5 us
    all_to_all x1, blocking collectives, on_device(): lax.all_to_all(outgoing, 'exp', split_axis=1, concat_axis=1, tiled=True)  27.9 us
  transfers between devices with their start and end apart: 5, of which 5 were waited for; matrix products, arithmetic and copies ran while one was open for 0% of the time, Pallas kernels for 0%

commit v1 on v0

v1 whole, which is shorter than its diff:
```python
import functools
import math

import jax
import jax.numpy as jnp
from jax import lax
from jax.experimental import pallas as pl
from jax.experimental.pallas import tpu as pltpu
from jax.sharding import PartitionSpec as P

STEPS = 2
LATENT = 512
VDIM = 128
TOPK = 8
CHIPS_X = 4
LANES = 128

qk_scale = 1.0 / math.sqrt(192.0)
norm_eps = 1e-06
MESH = pl.DeviceIdType.MESH
F32 = jnp.float32
BF16 = jnp.bfloat16
HIGH = lax.Precision.HIGHEST


def iota(shape, dim):
    return lax.broadcasted_iota(jnp.int32, shape, dim)


def log2(n):
    assert n & (n - 1) == 0
    return n.bit_length() - 1


def mm(a, b, precision=None):
    return jnp.dot(a, b, preferred_element_type=F32, precision=precision)


def mm_nt(a, b):
    return lax.dot_general(a, b, (((1,), (1,)), ((), ())), preferred_element_type=F32)


def far_first(n):
    return sorted(range(1, n), key=lambda k: (-min(k, n - k), k))


def pad_lanes(a, width):
    return jnp.concatenate([a, jnp.zeros((a.shape[0], width - a.shape[1]), a.dtype)], axis=1)


def pad_rows(a, height):
    return jnp.concatenate([a, jnp.zeros((height - a.shape[0], a.shape[1]), a.dtype)], axis=0)


class Plan:
    def __init__(self, nx, nz, ne, queries, cache, out_proj, gate_up):
        self.nx, self.nz, self.ne = nx, nz, ne
        self.rows = queries.shape[0]
        self.heads = queries.shape[2]
        self.width = queries.shape[3]
        self.span = cache.shape[1]
        self.hl = self.heads // (nx * nz)
        self.tok = self.rows * STEPS
        self.block = self.tok * self.hl
        self.total = self.tok * ne
        self.model = out_proj.shape[1]
        self.feat = self.model // (nx * nz)
        self.featp = -(-self.feat // LANES) * LANES
        self.vrows = out_proj.shape[0]
        self.ffe = gate_up.shape[2] // 2
        self.experts = gate_up.shape[0]
        self.nzz = nz // self.experts
        self.fb = self.ffe // (nx * self.nzz)
        self.base, at = {}, 0
        for name, n in (
            ("res", ne - 1),
            ("ax", nx - 1),
            ("axs", nx - 1),
            ("az", nz - 1),
            ("azs", nz - 1),
            ("b", ne - 1),
            ("core", nx),
            ("cx", nx - 1),
            ("cz", nz - 1),
            ("ce", ne - 1),
            ("sx", nx - 1),
            ("sz", nz - 1),
            ("ex", nx - 1),
            ("ez", nz - 1),
            ("gz", nz - 1),
            ("gx", nx - 1),
            ("f", ne - 1),
        ):
            self.base[name] = at
            at += n
        self.n_remote = at
        self.n_local = 2 * self.rows + 3 + self.experts * 2 * nx


def joined(stats):
    top = functools.reduce(jnp.maximum, [s[0:1, :] for s in stats])
    raw = [s[1:2, :] * jnp.exp(s[0:1, :] - top) for s in stats]
    total = functools.reduce(jnp.add, raw)
    inv = jnp.where(total > 0.0, 1.0 / jnp.where(total > 0.0, total, 1.0), 0.0)
    coefs = [r * inv for r in raw]
    width = top.shape[1]
    sub = iota((8, width), 0)
    packed = jnp.zeros((8, width), F32)
    for k, c in enumerate(coefs):
        packed = jnp.where(sub == k, c, packed)
    columns = jnp.transpose(pad_rows(packed, LANES))
    both = jnp.where(sub == 0, top, jnp.where(sub == 1, total, 0.0))
    return columns, both


def kernel(
    pn,
    q_hbm,
    nl_ref,
    cache_hbm,
    len_ref,
    vu_hbm,
    op_hbm,
    res_ref,
    gain_ref,
    ids_ref,
    rw_ref,
    gu_hbm,
    dn_hbm,
    out_ref,
    qs,
    ks,
    vus,
    ops,
    gus,
    dns,
    opw,
    rb,
    ra,
    os_,
    oxr,
    sxs,
    sxr,
    ozs,
    ozr,
    szs,
    szr,
    ctx_cols,
    ctz_cols,
    vs,
    vr,
    cs,
    cr,
    xs,
    xr,
    zs,
    zr,
    ys,
    yr,
    qxs,
    qxr,
    qzs,
    qzr,
    es,
    exr,
    ezs,
    ezr,
    act,
    fs,
    fr,
    send_sems,
    recv_sems,
    local_sems,
):
    nx, nz, ne = pn.nx, pn.nz, pn.ne
    ctx = lax.axis_index("ctx")
    me = lax.axis_index("exp")
    my_z, my_x = ctx // nx, lax.rem(ctx, nx)
    core = lax.rem(me, 2)
    pending = []

    def x_of(k):
        return lax.rem(my_x + k, nx)

    def z_of(k):
        return lax.rem(my_z + k, nz)

    def e_of(k):
        return lax.rem(me + k, ne)

    def x_dev(k):
        return (my_z * nx + x_of(k), me)

    def z_dev(k):
        return (z_of(k) * nx + my_x, me)

    def e_dev(k):
        return (ctx, e_of(k))

    core_dev = (ctx, me + 1 - 2 * core)

    def remote(src, dst, name, slot, dev):
        at = pn.base[name] + slot
        return pltpu.make_async_remote_copy(
            src_ref=src,
            dst_ref=dst,
            send_sem=send_sems.at[at],
            recv_sem=recv_sems.at[at],
            device_id=dev,
            device_id_type=MESH,
        )

    def send(src, dst, name, slot, dev):
        copy = remote(src, dst, name, slot, dev)
        copy.start()
        pending.append(copy)

    def receive(dst, name, slot, dev):
        remote(dst, dst, name, slot, dev).wait_recv()

    local_at = [0]

    def local(src, dst):
        copy = pltpu.make_async_copy(src, dst, local_sems.at[local_at[0]])
        local_at[0] += 1
        copy.start()
        return copy

    q_copies = [local(q_hbm.at[r], qs.at[r]) for r in range(pn.rows)]
    k_copies = [
        local(cache_hbm.at[r], ks.at[r, :, pl.ds(0, pn.span)]) for r in range(pn.rows)
    ]

    barrier = pltpu.get_barrier_semaphore()
    peers = (
        [x_dev(k) for k in range(1, nx)]
        + [z_dev(k) for k in range(1, nz)]
        + [e_dev(k) for k in range(1, ne)]
    )
    for dev in peers:
        pl.semaphore_signal(barrier, inc=1, device_id=dev, device_id_type=MESH)

    for r in range(pn.rows):
        fresh = pad_lanes(nl_ref[r].astype(F32), -(-pn.width // LANES) * LANES)
        fresh = jnp.transpose(pad_rows(fresh, LANES))[0 : pn.width, :]
        ks[r, :, pl.ds(pn.span, LANES)] = fresh.astype(BF16)
    res_rows = jnp.concatenate([res_ref[r].astype(F32) for r in range(pn.rows)], axis=0)
    rb[...] = pad_rows(pad_lanes(res_rows, pn.featp), 16).astype(BF16)
    ra[me] = rb[...]

    qrows = STEPS * pn.heads
    keys = pn.span + LANES
    m = iota((qrows, qrows), 0)
    lh, lz = log2(pn.hl), log2(nz)
    m_head = m & (pn.hl - 1)
    m_step = (m >> lh) & (STEPS - 1)
    m_z = (m >> (lh + 1)) & (nz - 1)
    m_x = m >> (lh + 1 + lz)
    source = m_step * pn.heads + (m_z * nx + m_x) * pn.hl + m_head
    perm = jnp.where(iota((qrows, qrows), 1) == source, 1.0, 0.0).astype(BF16)

    col = iota((qrows, keys), 1)
    step = (iota((qrows, keys), 0) >> lh) & (STEPS - 1)
    first = jnp.where(ctx == 0, 0, -LANES)
    is_fresh = (col >= pn.span) & (col - pn.span <= step + first)
    position = ctx * pn.span + col

    weight_copies = {}
    partial, peaks, denoms = [], [], []
    for r in range(pn.rows):
        q_copies[r].wait()
        k_copies[r].wait()
        if r == pn.rows - 1:
            weight_copies["vu"] = local(vu_hbm, vus)
            weight_copies["op"] = local(op_hbm, ops)
            for x in range(nx):
                for j in range(pn.experts):
                    for g in range(2):
                        at = g * pn.ffe + x * pn.nzz * pn.fb
                        weight_copies["gu", x, j, g] = local(
                            gu_hbm.at[j, :, pl.ds(at, pn.nzz * pn.fb)], gus.at[x, j, g]
                        )
            weight_copies["dn"] = local(dn_hbm, dns)
        qp = functools.reduce(
            jnp.add,
            [
                mm_nt(perm[:, s * pn.heads : (s + 1) * pn.heads], qs[r, s])
                for s in range(STEPS)
            ],
        ).astype(BF16)
        scores = mm(qp, ks[r])
        visible = ((col < pn.span) & (position < len_ref[r])) | is_fresh
        scores = jnp.where(visible, scores * qk_scale, -1e30)
        peak = jnp.max(scores, axis=1, keepdims=True)
        weights = jnp.where(visible, jnp.exp(scores - peak), 0.0)
        denom = jnp.sum(weights, axis=1, keepdims=True)
        mixture = mm_nt(weights.astype(BF16), ks[r, pl.ds(0, LATENT), :])
        inv = jnp.where(denom > 0.0, 1.0 / jnp.where(denom > 0.0, denom, 1.0), 0.0)
        partial.append(mixture * inv)
        peaks.append(peak)
        denoms.append(denom)

    pl.semaphore_wait(barrier, len(peers))

    half = STEPS * pn.hl
    groups = nx * nz
    merged = jnp.concatenate([p.reshape(groups, half, LATENT) for p in partial], axis=1)
    os_[...] = merged.astype(BF16).reshape(nx, nz, pn.block, LATENT)
    lane = iota((qrows, LANES), 1)
    stat = [
        jnp.where(lane == 0, p, jnp.where(lane == 1, d, 0.0)) for p, d in zip(peaks, denoms)
    ]
    stat = jnp.concatenate([s.reshape(groups, half, LANES) for s in stat], axis=1)
    stat = stat.reshape(nx, nz * pn.block, LANES)
    for x in range(nx):
        sxs[x] = jnp.transpose(stat[x])[0:8, :]
    for k in far_first(nx):
        xp = x_of(k)
        send(sxs.at[xp], sxr.at[k - 1], "axs", k - 1, x_dev(k))
        send(os_.at[xp], oxr.at[k - 1], "ax", k - 1, x_dev(k))
    for k in range(1, ne):
        send(rb, ra.at[me], "res", k - 1, e_dev(k))

    weight_copies["op"].wait()
    for z in range(nz):
        for x in range(nx):
            c = z * nx + x
            piece = ops[:, c * pn.feat : (c + 1) * pn.feat]
            opw[x, :, z * pn.featp : (z + 1) * pn.featp] = pad_lanes(piece, pn.featp)

    for k in range(1, nx):
        receive(sxr.at[k - 1], "axs", k - 1, x_dev(k))
    columns, both = joined([sxs[my_x]] + [sxr[k - 1] for k in range(1, nx)])
    ctx_cols[...] = columns
    szs[...] = both
    for k in range(1, nx):
        receive(oxr.at[k - 1], "ax", k - 1, x_dev(k))
    for k in far_first(nz) + [0]:
        zp = z_of(k)
        cols = ctx_cols[pl.ds(pl.multiple_of(zp * pn.block, pn.block), pn.block), :]
        acc = cols[:, 0:1] * os_[my_x, zp].astype(F32)
        for i in range(1, nx):
            acc = acc + cols[:, i : i + 1] * oxr[i - 1, zp].astype(F32)
        ozs[zp] = acc.astype(BF16)
        if k > 0:
            send(szs, szr.at[k - 1], "azs", k - 1, z_dev(k))
            send(ozs.at[zp], ozr.at[k - 1], "az", k - 1, z_dev(k))

    for k in range(1, ne):
        receive(ra.at[e_of(ne - k)], "res", k - 1, e_dev(k))
    lt, ly = log2(pn.tok), log2(ne // 2)

    def owner_of(n):
        y = (n >> lt) & (ne // 2 - 1)
        return 2 * y + (n >> (lt + ly)), n & (pn.tok - 1)

    n_row = iota((pn.total, ne * 16), 0)
    n_owner, n_tok = owner_of(n_row)
    spread = iota((pn.total, ne * 16), 1)
    pick = jnp.where(spread == n_owner * 16 + n_tok, 1.0, 0.0).astype(BF16)
    residual = mm(pick, ra[...].reshape(ne * 16, pn.featp))
    weight_copies["vu"].wait()

    for k in range(1, nz):
        receive(szr.at[k - 1], "azs", k - 1, z_dev(k))
    columns, _ = joined([szs[...]] + [szr[k - 1] for k in range(1, nz)])
    ctz_cols[...] = columns
    cols = ctz_cols[pl.ds(pl.multiple_of(my_z * pn.block, pn.block), pn.block), :]
    acc = cols[:, 0:1] * ozs[my_z].astype(F32)
    for k in range(1, nz):
        receive(ozr.at[k - 1], "az", k - 1, z_dev(k))
        acc = acc + cols[:, k : k + 1] * ozr[k - 1].astype(F32)
    latent_out = acc.astype(BF16)

    for i in range(pn.hl):
        vs[i] = mm(latent_out, vus[i]).astype(BF16)
    per_head = ne // pn.hl
    for k in range(1, ne):
        send(vs.at[e_of(k) // per_head], vr.at[me], "b", k - 1, e_dev(k))
    vr[me] = vs[me // per_head]
    place = n_tok * pn.hl + me // per_head
    value_pick = jnp.where(spread == n_owner * 16 + place, 1.0, 0.0).astype(BF16)
    for k in range(1, ne):
        receive(vr.at[e_of(ne - k)], "b", k - 1, e_dev(k))
    picked = mm(value_pick, vr[...].reshape(ne * 16, VDIM))
    values = picked[:, 0 : pn.vrows]
    for part in range(1, per_head):
        at = part * pn.vrows
        values = jnp.where(
            lax.rem(me, per_head) == part, picked[:, at : at + pn.vrows], values
        )
    values = values.astype(BF16)

    order = far_first(nx) + [0]
    hr = pn.total // 2
    for k in order:
        part = mm(values, opw[x_of(k)]).astype(BF16)
        cs[k, 0] = part[0:hr, :]
        cs[k, 1] = part[hr:, :]
        send(cs.at[k, 1 - core], cr.at[k], "core", k, core_dev)
    for k in order:
        receive(cr.at[k], "core", k, core_dev)
        for z in range(nz):
            at = slice(z * pn.featp, (z + 1) * pn.featp)
            xs[k, z] = (cs[k, core, :, at].astype(F32) + cr[k, :, at].astype(F32)).astype(BF16)
        if k > 0:
            send(xs.at[k], xr.at[k - 1], "cx", k - 1, x_dev(k))
    for k in range(1, nx):
        receive(xr.at[k - 1], "cx", k - 1, x_dev(k))
    for k in far_first(nz) + [0]:
        zp = z_of(k)
        acc = xs[0, zp].astype(F32)
        for i in range(1, nx):
            acc = acc + xr[i - 1, zp].astype(F32)
        zs[zp] = acc.astype(BF16)
        if k > 0:
            send(zs.at[zp], zr.at[k - 1], "cz", k - 1, z_dev(k))
    acc = zs[my_z].astype(F32)
    for k in range(1, nz):
        receive(zr.at[k - 1], "cz", k - 1, z_dev(k))
        acc = acc + zr[k - 1].astype(F32)
    ys[...] = acc.astype(BF16)
    yr[me] = ys[...]
    for k in range(1, ne):
        send(ys, yr.at[me], "ce", k - 1, e_dev(k))
    for k in range(1, ne):
        receive(yr.at[e_of(ne - k)], "ce", k - 1, e_dev(k))
    sides = []
    for c in range(2):
        acc = yr[c].astype(F32)
        for y in range(1, ne // 2):
            acc = acc + yr[2 * y + c].astype(F32)
        sides.append(acc)
    hidden = (residual + jnp.concatenate(sides, axis=0)).astype(BF16)
    hidden_f = hidden.astype(F32)

    squares = jnp.sum(hidden_f * hidden_f, axis=1, keepdims=True)
    squares = pad_rows(jnp.broadcast_to(squares, (pn.total, LANES)), LANES)
    qxs[...] = jnp.transpose(squares)[0:8, :]
    for k in far_first(nx):
        send(qxs, qxr.at[k - 1], "sx", k - 1, x_dev(k))
    scaled = (hidden_f[:, 0 : pn.feat] * gain_ref[...].reshape(1, pn.feat)).astype(BF16)
    for copy in [weight_copies[key] for key in weight_copies if key[0] == "gu"]:
        copy.wait()
    fb = pn.fb
    for k in order:
        xp = x_of(k)
        for j in range(pn.experts):
            for g in range(2):
                part = mm(scaled, gus[xp, j, g]).astype(BF16)
                for zz in range(pn.nzz):
                    es[k, j * pn.nzz + zz, :, g * fb : (g + 1) * fb] = part[
                        :, zz * fb : (zz + 1) * fb
                    ]
        if k > 0:
            send(es.at[k], exr.at[k - 1], "ex", k - 1, x_dev(k))
    acc = qxs[...]
    for k in range(1, nx):
        receive(qxr.at[k - 1], "sx", k - 1, x_dev(k))
        acc = acc + qxr[k - 1]
    qzs[...] = acc
    for k in far_first(nz):
        send(qzs, qzr.at[k - 1], "sz", k - 1, z_dev(k))
    for k in range(1, nx):
        receive(exr.at[k - 1], "ex", k - 1, x_dev(k))
    for k in far_first(nz) + [0]:
        zp = z_of(k)
        acc = es[0, zp].astype(F32)
        for i in range(1, nx):
            acc = acc + exr[i - 1, zp].astype(F32)
        ezs[zp] = acc.astype(BF16)
        if k > 0:
            send(ezs.at[zp], ezr.at[k - 1], "ez", k - 1, z_dev(k))
    acc = qzs[...]
    for k in range(1, nz):
        receive(qzr.at[k - 1], "sz", k - 1, z_dev(k))
        acc = acc + qzr[k - 1]
    scale_row = lax.rsqrt(acc / pn.model + norm_eps)
    scale = jnp.transpose(pad_rows(scale_row, LANES))[0 : pn.total, 0:1]
    acc = ezs[my_z].astype(F32)
    for k in range(1, nz):
        receive(ezr.at[k - 1], "ez", k - 1, z_dev(k))
        acc = acc + ezr[k - 1].astype(F32)
    acc = acc * scale
    gate, up = acc[:, 0:fb], acc[:, fb : 2 * fb]
    activated = gate / (1.0 + jnp.exp(-gate)) * up
    act[my_x, my_z] = activated.astype(BF16)

    for k in far_first(nz):
        send(act.at[my_x, my_z], act.at[my_x, my_z], "gz", k - 1, z_dev(k))
    weight_copies["dn"].wait()
    for k in range(1, nz):
        receive(act.at[my_x, z_of(nz - k)], "gz", k - 1, z_dev(k))
    for k in far_first(nx):
        send(act.at[my_x], act.at[my_x], "gx", k - 1, x_dev(k))
    depth = pn.nzz * fb
    outs = [jnp.zeros((pn.total, pn.feat), F32) for _ in range(pn.experts)]
    for k in range(nx):
        xp = x_of(nx - k)
        if k > 0:
            receive(act.at[xp], "gx", k - 1, x_dev(k))
        for j in range(pn.experts):
            rows = jnp.concatenate(
                [act[xp, j * pn.nzz + zz] for zz in range(pn.nzz)], axis=1
            )
            down = dns[j, :, pl.ds(pl.multiple_of(xp * depth, depth), depth)]
            outs[j] = outs[j] + mm_nt(rows, down)

    s_row = iota((ne * 16, pn.total), 0)
    s_owner, s_tok = owner_of(iota((ne * 16, pn.total), 1))
    acc = jnp.zeros((ne * 16, pn.featp), F32)
    for j in range(pn.experts):
        put = jnp.where(s_row == s_owner * 16 + j * pn.tok + s_tok, 1.0, 0.0).astype(BF16)
        acc = acc + mm(put, pad_lanes(outs[j], pn.featp).astype(BF16))
    fs[...] = acc.astype(BF16).reshape(ne, 16, pn.featp)
    for k in range(1, ne):
        send(fs.at[e_of(k)], fr.at[me], "f", k - 1, e_dev(k))
    fr[me] = fs[me]

    ids = pad_rows(
        jnp.concatenate([ids_ref[r] for r in range(pn.rows)], axis=0), 8
    )
    coef = pad_rows(jnp.concatenate([rw_ref[r] for r in range(pn.rows)], axis=0), 8)
    c_row, c_col = iota((8, ne * 16), 0), iota((8, ne * 16), 1)
    place = c_col & 15
    expert = (c_col >> 4) * pn.experts + (place >> lt)
    used = (place < pn.experts * pn.tok) & ((place & (pn.tok - 1)) == c_row)
    mix = jnp.zeros((8, ne * 16), F32)
    for t in range(TOPK):
        mix = mix + jnp.where(used & (expert == ids[:, t : t + 1]), coef[:, t : t + 1], 0.0)
    own_row, own_col = iota((8, pn.total), 0), iota((8, pn.total), 1)
    own_at = core * hr + (me // 2) * pn.tok + own_row
    own = jnp.where((own_col == own_at) & (own_row < pn.tok), 1.0, 0.0).astype(BF16)
    own_hidden = mm(own, hidden)

    for k in range(1, ne):
        receive(fr.at[e_of(ne - k)], "f", k - 1, e_dev(k))
    returned = fr[...].reshape(ne * 16, pn.featp).astype(F32)
    mixed = own_hidden + mm(mix, returned, HIGH)
    for r in range(pn.rows):
        out_ref[r] = mixed[r * STEPS : (r + 1) * STEPS, 0 : pn.feat].astype(BF16)
    for copy in pending:
        copy.wait_send()


def on_device(
    nx,
    queries,
    new_latent,
    cache,
    lengths,
    value_up,
    out_proj,
    residual,
    norm_gain,
    route_ids,
    route_weights,
    gate_up,
    expert_down,
):
    ne = lax.axis_size("exp")
    nz = lax.axis_size("ctx") // nx
    pn = Plan(nx, nz, ne, queries, cache, out_proj, gate_up)
    keys = pn.span + LANES
    stat_lanes = nz * pn.block
    any_spec = pl.BlockSpec(memory_space=pl.ANY)
    vmem_spec = pl.BlockSpec(memory_space=pltpu.VMEM)
    smem_spec = pl.BlockSpec(memory_space=pltpu.SMEM)
    fp, total = pn.featp, pn.total
    v = pltpu.VMEM
    scratch = [
        v((pn.rows, STEPS, pn.width, pn.heads), BF16),
        v((pn.rows, pn.width, keys), BF16),
        v(value_up.shape, BF16),
        v(out_proj.shape, BF16),
        v((nx, pn.experts, 2, pn.feat, pn.nzz * pn.fb), BF16),
        v((pn.experts, pn.feat, pn.ffe), BF16),
        v((nx, pn.vrows, nz * fp), BF16),
        v((16, fp), BF16),
        v((ne, 16, fp), BF16),
        v((nx, nz, pn.block, LATENT), BF16),
        v((nx - 1, nz, pn.block, LATENT), BF16),
        v((nx, 8, stat_lanes), F32),
        v((nx - 1, 8, stat_lanes), F32),
        v((nz, pn.block, LATENT), BF16),
        v((nz - 1, pn.block, LATENT), BF16),
        v((8, stat_lanes), F32),
        v((nz - 1, 8, stat_lanes), F32),
        v((stat_lanes, LANES), F32),
        v((stat_lanes, LANES), F32),
        v((pn.hl, pn.block, VDIM), BF16),
        v((ne, pn.block, VDIM), BF16),
        v((nx, 2, total // 2, nz * fp), BF16),
        v((nx, total // 2, nz * fp), BF16),
        v((nx, nz, total // 2, fp), BF16),
        v((nx - 1, nz, total // 2, fp), BF16),
        v((nz, total // 2, fp), BF16),
        v((nz - 1, total // 2, fp), BF16),
        v((total // 2, fp), BF16),
        v((ne, total // 2, fp), BF16),
        v((8, LANES), F32),
        v((nx - 1, 8, LANES), F32),
        v((8, LANES), F32),
        v((nz - 1, 8, LANES), F32),
        v((nx, nz, total, 2 * pn.fb), BF16),
        v((nx - 1, nz, total, 2 * pn.fb), BF16),
        v((nz, total, 2 * pn.fb), BF16),
        v((nz - 1, total, 2 * pn.fb), BF16),
        v((nx, nz, total, pn.fb), BF16),
        v((ne, 16, fp), BF16),
        v((ne, 16, fp), BF16),
        pltpu.SemaphoreType.DMA((pn.n_remote,)),
        pltpu.SemaphoreType.DMA((pn.n_remote,)),
        pltpu.SemaphoreType.DMA((pn.n_local,)),
    ]
    return pl.pallas_call(
        functools.partial(kernel, pn),
        out_shape=jax.ShapeDtypeStruct(residual.shape, BF16),
        in_specs=[
            any_spec,
            vmem_spec,
            any_spec,
            smem_spec,
            any_spec,
            any_spec,
            vmem_spec,
            vmem_spec,
            vmem_spec,
            vmem_spec,
            any_spec,
            any_spec,
        ],
        out_specs=vmem_spec,
        scratch_shapes=scratch,
        compiler_params=pltpu.CompilerParams(
            collective_id=0, has_side_effects=True, vmem_limit_bytes=60 * 1024 * 1024
        ),
        name="decode_layer",
    )(
        jnp.swapaxes(queries, 2, 3),
        new_latent,
        jnp.swapaxes(cache, 1, 2),
        lengths,
        value_up,
        out_proj,
        residual,
        norm_gain,
        route_ids,
        route_weights,
        gate_up,
        jnp.swapaxes(expert_down, 1, 2),
    )


def solution(mesh, nx=CHIPS_X):
    in_specs = (
        P("exp", None, None, None),
        P("exp", None, None),
        P("exp", "ctx", None),
        P("exp"),
        P("ctx", None, None),
        P(("ctx", "exp"), None),
        P("exp", None, "ctx"),
        P("ctx"),
        P("exp", None, None),
        P("exp", None, None),
        P("exp", "ctx", None),
        P("exp", None, "ctx"),
    )
    return jax.shard_map(
        functools.partial(on_device, nx),
        mesh=mesh,
        in_specs=in_specs,
        out_specs=P("exp", None, "ctx"),
        check_vma=False,
    )
```

time: 853 us -> 77.1 us (0.09)
  waiting for transfers between devices: 576 us -> 0 us
  blocking collectives: 179 us -> 0 us
  Pallas kernels: 0 us -> 75.7 us
  other arithmetic: 50.2 us -> 0 us
  between operations: 14 us -> 0.01 us
  matrix products: 13 us -> 0 us
  starting transfers between devices: 9.68 us -> 0 us
    unnamed x6 -> x0, waiting for transfers between devices: 276 us -> none
    all_gather x1 -> x0, waiting for transfers between devices: 155 us -> none  [combined_all(): gathered = jax.tree.map(lambda a: lax.all_gather(a, axis), part)]
    psum x1 -> x0, waiting for transfers between devices: 141 us -> none  [on_device(): gate_up_sum = lax.psum(gate_up_sum, 'ctx')]
    all_gather x2 -> x0, blocking collectives: 82.3 us -> none  [combined_all(): gathered = jax.tree.map(lambda a: lax.all_gather(a, axis), part)]
    pallas_call x0 -> x1, Pallas kernels: none -> 75.7 us  [on_device(): pl.pallas_call(functools.partial(kernel, pn), out_shape=jax.ShapeDtypeStr...]
    psum x1 -> x0, blocking collectives: 58.8 us -> none  [on_device(): squares = lax.psum(jnp.sum(hidden_f * hidden_f, axis=1), 'ctx')]
    add x64 -> x0, other arithmetic: 48.3 us -> none  [the longest x31 47.5 us: join_parts(): left_part[0] * left_scale[..., None]]
    all_to_all x2 -> x0, blocking collectives: 37.6 us -> none  [the longest x1 27.9 us: on_device(): lax.all_to_all(outgoing, 'exp', split_axis=1, concat_axis=1, tiled=True)]
  transfers between devices with their start and end apart: 5 -> 0, of which waited for: 5 -> 0; matrix products, arithmetic and copies ran while one was open for 0% -> 0% of each run, Pallas kernels for 0% -> 0%
where the time goes in v1:
time: 77.1 us; the launch traced here: 76.9 us
  Pallas kernels  75.7 us (98%)
  local copies, waits for them, and re-layouts  1.26 us (2%)
    pallas_call x1, Pallas kernels, on_device(): pl.pallas_call(functools.partial(kernel, pn), out_shape=jax.ShapeDtypeStr...  75.7 us

profile of v1, /device:TPU:1, one launch (start us, length us, event | category | flops | bytes accessed | tf_op | source)
XLA Modules:
  0.0 76.9 jit_solution(9713827009131058182)
XLA Ops:
  0.0 75.7 %decode_layer.1 = bf16[2,2,224]{2,1,0:T(2,128)(2,1)} custom-call(bf16[2,2,576,128]{3,2,1,0:T(8,128)(2,1)} %bitcast.5, bf16[2,2,576]{2,1,0:T(2,128)(2,1)} %nl_ref.1, bf16[2,576,512]{2,1,0:T(8,128)(2,1)} %bitcast.4, s32[2]{0:T(128)} %len_ref.1, bf16[4,512,128]{2,1,0:T(8,128)(2,1)} %vu_hbm.1, bf16[64,7168]{1,0:T(8,128)(2,1)} %op_hbm.1, ...), custom_call_target="tpu_custom_call" | custom-call | tf_op jit(solution)/shard_map/decode_layer/pallas_call | solution.py:616
  75.7 1.3 %copy.14 = bf16[2,2,224]{2,1,0:T(2,128)(2,1)} copy(bf16[2,2,224]{2,1,0:T(2,128)(2,1)} %decode_layer.1) | data formatting | bytes 3584

commit v2 on v1

v2 whole, which is shorter than its diff:
```python
import functools
import math

import jax
import jax.numpy as jnp
from jax import lax
from jax.experimental import pallas as pl
from jax.experimental.pallas import tpu as pltpu
from jax.sharding import PartitionSpec as P

STEPS = 2
LATENT = 512
VDIM = 128
TOPK = 8
CHIPS_X = 4
LANES = 128

qk_scale = 1.0 / math.sqrt(192.0)
norm_eps = 1e-06
MESH = pl.DeviceIdType.MESH
F32 = jnp.float32
BF16 = jnp.bfloat16
HIGH = lax.Precision.HIGHEST


def iota(shape, dim):
    return lax.broadcasted_iota(jnp.int32, shape, dim)


def log2(n):
    assert n & (n - 1) == 0
    return n.bit_length() - 1


def mm(a, b, precision=None):
    return jnp.dot(a, b, preferred_element_type=F32, precision=precision)


def mm_nt(a, b):
    return lax.dot_general(a, b, (((1,), (1,)), ((), ())), preferred_element_type=F32)


def far_first(n):
    return sorted(range(1, n), key=lambda k: (-min(k, n - k), k))


def pad_lanes(a, width):
    return jnp.concatenate([a, jnp.zeros((a.shape[0], width - a.shape[1]), a.dtype)], axis=1)


def pad_rows(a, height):
    return jnp.concatenate([a, jnp.zeros((height - a.shape[0], a.shape[1]), a.dtype)], axis=0)


class Plan:
    def __init__(self, nx, nz, ne, queries, cache, out_proj, gate_up):
        self.nx, self.nz, self.ne, self.ny = nx, nz, ne, ne // 2
        self.rows = queries.shape[0]
        self.heads = queries.shape[2]
        self.width = queries.shape[3]
        self.span = cache.shape[1]
        self.hl = self.heads // (nx * nz)
        assert self.hl == self.ny
        self.tok = self.rows * STEPS
        self.block = self.tok * self.hl
        self.total = self.tok * ne
        self.model = out_proj.shape[1]
        self.feat = self.model // (nx * nz)
        self.featp = -(-self.feat // LANES) * LANES
        self.vrows = out_proj.shape[0]
        self.ffe = gate_up.shape[2] // 2
        self.experts = gate_up.shape[0]
        self.nzz = nz // self.experts
        self.fb = self.ffe // (nx * self.nzz)
        self.zorder = far_first(nz) + [0]
        self.xorder = far_first(nx) + [0]
        self.halves = 2
        self.per = nz // self.halves
        nxy = nx * self.ny - 1
        self.base, at = {}, 0
        for name, n in (
            ("res", ne - 1),
            ("op", 1),
            ("as", nxy),
            ("a", nxy * self.halves),
            ("azs", nz - 1),
            ("az", nz - 1),
            ("cx", (nx - 1) * self.halves),
            ("cz", nz - 1),
            ("ce", ne - 1),
            ("sx", nx - 1),
            ("sz", nz - 1),
            ("ex", (nx - 1) * self.halves),
            ("ez", nz - 1),
            ("gz", nz - 1),
            ("gx", (nx - 1) * nz),
            ("f", ne - 1),
        ):
            self.base[name] = at
            at += n
        self.n_remote = at
        self.n_local = 2 * self.rows + 10


def joined(tops, totals):
    top = functools.reduce(jnp.maximum, tops)
    raw = [d * jnp.exp(p - top) for p, d in zip(tops, totals)]
    total = functools.reduce(jnp.add, raw)
    inv = jnp.where(total > 0.0, 1.0 / jnp.where(total > 0.0, total, 1.0), 0.0)
    return [r * inv for r in raw], top, total


def kernel(
    pn,
    q_hbm,
    nl_hbm,
    cache_hbm,
    len_hbm,
    vu_hbm,
    op_hbm,
    res_hbm,
    gain_ref,
    ids_hbm,
    rw_hbm,
    gu_hbm,
    dn_hbm,
    out_ref,
    nl_ref,
    len_ref,
    res_ref,
    ids_ref,
    rw_ref,
    qs,
    ks,
    vus,
    ops,
    gus,
    dns,
    opw,
    rb,
    ra,
    os_,
    oxr,
    sxs,
    sxr,
    ozs,
    ozr,
    szs,
    szr,
    xy_cols,
    cs,
    cr,
    zs,
    zr,
    ys,
    yr,
    qxs,
    qxr,
    qzs,
    qzr,
    es,
    exr,
    ezs,
    ezr,
    act,
    fs,
    fr,
    send_sems,
    recv_sems,
    local_sems,
):
    nx, ny, nz, ne = pn.nx, pn.ny, pn.nz, pn.ne
    halves, per = pn.halves, pn.per
    zorder, xorder = pn.zorder, pn.xorder
    ctx = lax.axis_index("ctx")
    me = lax.axis_index("exp")
    my_z, my_x = ctx // nx, lax.rem(ctx, nx)
    my_y, core = me // 2, lax.rem(me, 2)
    pending = []

    def x_of(k):
        return lax.rem(my_x + k, nx)

    def y_of(k):
        return lax.rem(my_y + k, ny)

    def z_of(k):
        return lax.rem(my_z + k, nz)

    def e_of(k):
        return lax.rem(me + k, ne)

    def x_dev(k):
        return (my_z * nx + x_of(k), me)

    def xy_dev(kx, ky):
        return (my_z * nx + x_of(kx), 2 * y_of(ky) + core)

    def z_dev(k):
        return (z_of(k) * nx + my_x, me)

    def e_dev(k):
        return (ctx, e_of(k))

    core_dev = (ctx, me + 1 - 2 * core)

    xy_far = [
        (kx, ky) for kx in far_first(nx) + [0] for ky in far_first(ny) + [0] if kx or ky
    ]
    barrier = pltpu.get_barrier_semaphore()
    peers = (
        [z_dev(k) for k in far_first(nz)]
        + [xy_dev(kx, ky) for kx, ky in xy_far]
        + [(ctx, 2 * y_of(ky) + 1 - core) for ky in range(ny)]
    )
    for dev in peers:
        pl.semaphore_signal(barrier, inc=1, device_id=dev, device_id_type=MESH)

    def remote(src, dst, name, slot, dev):
        at = pn.base[name] + slot
        return pltpu.make_async_remote_copy(
            src_ref=src,
            dst_ref=dst,
            send_sem=send_sems.at[at],
            recv_sem=recv_sems.at[at],
            device_id=dev,
            device_id_type=MESH,
        )

    def send(src, dst, name, slot, dev):
        copy = remote(src, dst, name, slot, dev)
        copy.start()
        pending.append(copy)

    def receive(dst, name, slot, dev):
        remote(dst, dst, name, slot, dev).wait_recv()

    local_at = [0]

    def local(src, dst):
        copy = pltpu.make_async_copy(src, dst, local_sems.at[local_at[0]])
        local_at[0] += 1
        copy.start()
        return copy

    q_copies = [local(q_hbm.at[r], qs.at[r]) for r in range(pn.rows)]
    k_copies = [
        local(cache_hbm.at[r], ks.at[r, :, pl.ds(0, pn.span)]) for r in range(pn.rows)
    ]
    small_copies = [
        local(nl_hbm, nl_ref),
        local(len_hbm, len_ref),
        local(res_hbm, res_ref),
        local(ids_hbm, ids_ref),
        local(rw_hbm, rw_ref),
    ]
    op_copy = local(op_hbm, ops.at[core])
    vu_copy = local(vu_hbm.at[my_y], vus)

    qrows = STEPS * pn.heads
    keys = pn.span + LANES
    lp, lh, lhl = log2(per), log2(halves), log2(pn.hl)
    m = iota((qrows, qrows), 0)
    m_place = (m >> 1) & (nz - 1)
    m_head = (m >> (1 + lp + lh)) & (pn.hl - 1)
    m_x = m >> (1 + lp + lh + lhl)
    m_z = jnp.zeros_like(m)
    for place, k in enumerate(zorder):
        m_z = jnp.where(m_place == place, z_of(k), m_z)
    source = (m & (STEPS - 1)) * pn.heads + (m_z * nx + m_x) * pn.hl + m_head
    perm = jnp.where(iota((qrows, qrows), 1) == source, 1.0, 0.0).astype(BF16)

    col = iota((qrows, keys), 1)
    step = iota((qrows, keys), 0) & (STEPS - 1)
    first = jnp.where(ctx == 0, 0, -LANES)
    is_fresh = (col >= pn.span) & (col - pn.span <= step + first)
    position = ctx * pn.span + col

    for copy in small_copies:
        copy.wait()
    for r in range(pn.rows):
        fresh = pad_lanes(nl_ref[r].astype(F32), -(-pn.width // LANES) * LANES)
        fresh = jnp.transpose(pad_rows(fresh, LANES))[0 : pn.width, :]
        ks[r, :, pl.ds(pn.span, LANES)] = fresh.astype(BF16)
    res_rows = jnp.concatenate([res_ref[r].astype(F32) for r in range(pn.rows)], axis=0)
    rb[...] = pad_rows(pad_lanes(res_rows, pn.featp), 16).astype(BF16)
    ra[me] = rb[...]

    gu_sem, dn_copy = local_sems.at[pn.n_local - 1], None
    partial, peaks, denoms = [], [], []
    for r in range(pn.rows):
        q_copies[r].wait()
        k_copies[r].wait()
        if r == pn.rows - 1:
            for x in range(nx):
                for z in range(nz):
                    j, zz = z // pn.nzz, z % pn.nzz
                    for g in range(2):
                        at = g * pn.ffe + (x * pn.nzz + zz) * pn.fb
                        pltpu.make_async_copy(
                            gu_hbm.at[j, :, pl.ds(at, pn.fb)],
                            gus.at[x, z, :, pl.ds(g * pn.fb, pn.fb)],
                            gu_sem,
                        ).start()
            dn_copy = local(dn_hbm, dns)
        qp = functools.reduce(
            jnp.add,
            [
                mm_nt(perm[:, s * pn.heads : (s + 1) * pn.heads], qs[r, s])
                for s in range(STEPS)
            ],
        ).astype(BF16)
        scores = mm(qp, ks[r])
        visible = ((col < pn.span) & (position < len_ref[r])) | is_fresh
        scores = jnp.where(visible, scores * qk_scale, -1e30)
        peak = jnp.max(scores, axis=1, keepdims=True)
        weights = jnp.where(visible, jnp.exp(scores - peak), 0.0)
        denom = jnp.sum(weights, axis=1, keepdims=True)
        mixture = mm_nt(weights.astype(BF16), ks[r, pl.ds(0, LATENT), :])
        inv = jnp.where(denom > 0.0, 1.0 / jnp.where(denom > 0.0, denom, 1.0), 0.0)
        partial.append(mixture * inv)
        peaks.append(peak)
        denoms.append(denom)

    span_rows = STEPS * per
    groups = nx * pn.hl * halves
    lane = iota((qrows, LANES), 1)
    stat = [
        jnp.where(lane == 0, p, jnp.where(lane == 1, d, 0.0)) for p, d in zip(peaks, denoms)
    ]
    stat = jnp.concatenate([s.reshape(groups, span_rows, LANES) for s in stat], axis=1)
    stat = stat.reshape(nx, nz * pn.block, LANES)
    for x in range(nx):
        sxs[x] = jnp.transpose(stat[x])[0:8, :]
    sxr[0, my_y] = sxs[my_x]
    crow = pn.rows * span_rows
    merged = jnp.concatenate(
        [p.reshape(groups, span_rows, LATENT) for p in partial], axis=1
    )
    os_[...] = merged.astype(BF16).reshape(nx, pn.hl, halves, crow, LATENT)
    oxr[0, my_y] = os_[my_x, my_y]

    pl.semaphore_wait(barrier, len(peers))
    for kx, ky in xy_far:
        slot = kx * ny + ky - 1
        send(sxs.at[x_of(kx)], sxr.at[kx, my_y], "as", slot, xy_dev(kx, ky))
    for h in range(halves):
        for kx, ky in xy_far:
            slot = (kx * ny + ky - 1) * halves + h
            send(
                os_.at[x_of(kx), y_of(ky), h],
                oxr.at[kx, my_y, h],
                "a",
                slot,
                xy_dev(kx, ky),
            )
    op_copy.wait()
    send(ops.at[core], ops.at[core], "op", 0, core_dev)
    for k in range(1, ne):
        send(rb, ra.at[me], "res", k - 1, e_dev(k))

    for kx, ky in reversed(xy_far):
        src_y = y_of(ny - ky)
        receive(sxr.at[kx, src_y], "as", kx * ny + ky - 1, xy_dev(kx, ky))
    tops = [
        jnp.concatenate([sxr[kx, y, 0:1, :] for y in range(ny)], axis=0) for kx in range(nx)
    ]
    totals = [
        jnp.concatenate([sxr[kx, y, 1:2, :] for y in range(ny)], axis=0) for kx in range(nx)
    ]
    coefs, top, total = joined(tops, totals)
    table = pad_rows(jnp.concatenate(coefs + [top, total], axis=0), LANES)
    xy_cols[...] = jnp.transpose(table)
    mine = halves * crow
    cols = xy_cols[pl.ds(pl.multiple_of(my_y * mine, mine), mine), :]

    hrows = ny * crow
    lrow, ly = log2(pn.rows), log2(ny)
    a = iota((hrows, hrows), 0)
    a_step, a_row = a & 1, (a >> 1) & (pn.rows - 1)
    a_y, a_place = (a >> (1 + lrow)) & (ny - 1), a >> (1 + lrow + ly)
    a_from = a_y * crow + a_row * span_rows + a_place * STEPS + a_step
    turn = jnp.where(iota((hrows, hrows), 1) == a_from, 1.0, 0.0)
    lane = iota((crow, LANES), 1)
    stat = []
    for h in range(halves):
        at = slice(h * crow, (h + 1) * crow)
        rows = [
            jnp.where(
                lane == 0,
                cols[at, nx * ny + y : nx * ny + y + 1],
                jnp.where(lane == 1, cols[at, (nx + 1) * ny + y : (nx + 1) * ny + y + 1], 0.0),
            )
            for y in range(ny)
        ]
        stat.append(mm(turn, jnp.concatenate(rows, axis=0), HIGH))
    szs[...] = jnp.transpose(jnp.concatenate(stat, axis=0))[0:8, :]
    for k in far_first(nz):
        send(szs, szr.at[k - 1], "azs", k - 1, z_dev(k))
    turn = turn.astype(BF16)
    for h in range(halves):
        for kx, ky in reversed(xy_far):
            slot = (kx * ny + ky - 1) * halves + h
            receive(oxr.at[kx, y_of(ny - ky), h], "a", slot, xy_dev(kx, ky))
        at = slice(h * crow, (h + 1) * crow)
        sums = []
        for y in range(ny):
            acc = cols[at, y : y + 1] * oxr[0, y, h].astype(F32)
            for kx in range(1, nx):
                c = kx * ny + y
                acc = acc + cols[at, c : c + 1] * oxr[kx, y, h].astype(F32)
            sums.append(acc.astype(BF16))
        turned = mm(turn, jnp.concatenate(sums, axis=0)).astype(BF16)
        for p in range(per):
            place = h * per + p
            ozs[place] = turned[p * pn.block : (p + 1) * pn.block, :]
            k = zorder[place]
            if k > 0:
                send(ozs.at[place], ozr.at[k - 1], "az", k - 1, z_dev(k))

    receive(ops.at[1 - core], "op", 0, core_dev)
    for z in range(nz):
        for x in range(nx):
            c = z * nx + x
            for half in range(2):
                piece = ops[half, :, c * pn.feat : (c + 1) * pn.feat]
                opw[x, z, half * pn.vrows : (half + 1) * pn.vrows, :] = pad_lanes(
                    piece, pn.featp
                )
    for k in range(1, ne):
        receive(ra.at[e_of(ne - k)], "res", k - 1, e_dev(k))
    lt = log2(pn.tok)

    def owner_of(n):
        y = (n >> lt) & (ny - 1)
        return 2 * y + (n >> (lt + ly)), n & (pn.tok - 1)

    n_row = iota((pn.total, ne * 16), 0)
    n_owner, n_tok = owner_of(n_row)
    spread = iota((pn.total, ne * 16), 1)
    pick = jnp.where(spread == n_owner * 16 + n_tok, 1.0, 0.0).astype(BF16)
    residual = mm(pick, ra[...].reshape(ne * 16, pn.featp))
    vu_copy.wait()

    def stat_of(ref, k):
        at = zorder.index(k) * pn.block
        return pad_lanes(ref[0:2, at : at + pn.block], LANES)

    for k in range(1, nz):
        receive(szr.at[k - 1], "azs", k - 1, z_dev(k))
    stat = [stat_of(szs, 0)] + [stat_of(szr.at[k - 1], k) for k in range(1, nz)]
    coefs, _, _ = joined([s[0:1, :] for s in stat], [s[1:2, :] for s in stat])
    cols = jnp.transpose(pad_rows(jnp.concatenate(coefs, axis=0), LANES))[0 : pn.block, :]
    acc = cols[:, 0:1] * ozs[nz - 1].astype(F32)
    for k in reversed(far_first(nz)):
        receive(ozr.at[k - 1], "az", k - 1, z_dev(k))
        acc = acc + cols[:, k : k + 1] * ozr[k - 1].astype(F32)
    values = mm(acc.astype(BF16), vus[...]).astype(BF16)

    def partner_chunk(h):
        return pl.ds(h * per, per)

    for h in range(halves):
        for k in xorder:
            for p in range(per):
                place = h * per + p
                block = mm(values, opw[x_of(k), z_of(zorder[place])])
                cs[k, place] = block.astype(BF16)
            if k > 0:
                send(
                    cs.at[k, partner_chunk(h)],
                    cr.at[k - 1, partner_chunk(h)],
                    "cx",
                    (k - 1) * halves + h,
                    x_dev(k),
                )
    for h in range(halves):
        for k in range(1, nx):
            receive(
                cr.at[k - 1, partner_chunk(h)], "cx", (k - 1) * halves + h, x_dev(k)
            )
        for p in range(per):
            place = h * per + p
            acc = cs[0, place].astype(F32)
            for i in range(1, nx):
                acc = acc + cr[i - 1, place].astype(F32)
            zs[place] = acc.astype(BF16)
            k = zorder[place]
            if k > 0:
                send(zs.at[place], zr.at[k - 1], "cz", k - 1, z_dev(k))
    acc = zs[nz - 1].astype(F32)
    for k in reversed(far_first(nz)):
        receive(zr.at[k - 1], "cz", k - 1, z_dev(k))
        acc = acc + zr[k - 1].astype(F32)
    ys[...] = acc.astype(BF16)
    for k in far_first(ne):
        send(ys, yr.at[me], "ce", k - 1, e_dev(k))
    yr[me] = ys[...]
    for k in range(1, ne):
        receive(yr.at[e_of(ne - k)], "ce", k - 1, e_dev(k))
    sides = []
    for c in range(2):
        acc = yr[c].astype(F32)
        for y in range(1, ny):
            acc = acc + yr[2 * y + c].astype(F32)
        sides.append(acc)
    hidden = (residual + jnp.concatenate(sides, axis=0)).astype(BF16)
    hidden_f = hidden.astype(F32)

    scaled = (hidden_f[:, 0 : pn.feat] * gain_ref[...].reshape(1, pn.feat)).astype(BF16)
    pltpu.make_async_copy(gus, gus, gu_sem).wait()
    fb = pn.fb
    for h in range(halves):
        for k in xorder:
            for p in range(per):
                place = h * per + p
                block = mm(scaled, gus[x_of(k), z_of(zorder[place])])
                es[k, place] = block.astype(BF16)
            if k > 0:
                send(
                    es.at[k, partner_chunk(h)],
                    exr.at[k - 1, partner_chunk(h)],
                    "ex",
                    (k - 1) * halves + h,
                    x_dev(k),
                )
        if h == 0:
            squares = jnp.sum(hidden_f * hidden_f, axis=1, keepdims=True)
            squares = pad_rows(jnp.broadcast_to(squares, (pn.total, LANES)), LANES)
            qxs[...] = jnp.transpose(squares)[0:8, :]
            for k in far_first(nx):
                send(qxs, qxr.at[k - 1], "sx", k - 1, x_dev(k))
    acc = qxs[...]
    for k in range(1, nx):
        receive(qxr.at[k - 1], "sx", k - 1, x_dev(k))
        acc = acc + qxr[k - 1]
    qzs[...] = acc
    for h in range(halves):
        for k in range(1, nx):
            receive(
                exr.at[k - 1, partner_chunk(h)], "ex", (k - 1) * halves + h, x_dev(k)
            )
        for p in range(per):
            place = h * per + p
            acc = es[0, place].astype(F32)
            for i in range(1, nx):
                acc = acc + exr[i - 1, place].astype(F32)
            ezs[place] = acc.astype(BF16)
            k = zorder[place]
            if k > 0:
                send(ezs.at[place], ezr.at[k - 1], "ez", k - 1, z_dev(k))
                send(qzs, qzr.at[k - 1], "sz", k - 1, z_dev(k))
    acc = qzs[...]
    for k in range(1, nz):
        receive(qzr.at[k - 1], "sz", k - 1, z_dev(k))
        acc = acc + qzr[k - 1]
    scale_row = lax.rsqrt(acc / pn.model + norm_eps)
    scale = jnp.transpose(pad_rows(scale_row, LANES))[0 : pn.total, 0:1]
    acc = ezs[nz - 1].astype(F32)
    for k in reversed(far_first(nz)):
        receive(ezr.at[k - 1], "ez", k - 1, z_dev(k))
        acc = acc + ezr[k - 1].astype(F32)
    acc = acc * scale
    gate, up = acc[:, 0:fb], acc[:, fb : 2 * fb]
    activated = gate / (1.0 + jnp.exp(-gate)) * up
    act[my_x, my_z] = activated.astype(BF16)

    for k in far_first(nz):
        send(act.at[my_x, my_z], act.at[my_x, my_z], "gz", k - 1, z_dev(k))
    dn_copy.wait()
    for k in [0] + list(reversed(far_first(nz))):
        block = act.at[my_x, z_of(nz - k)]
        if k > 0:
            receive(block, "gz", k - 1, z_dev(k))
        for i in far_first(nx):
            send(block, block, "gx", (i - 1) * nz + k, x_dev(i))
    depth = pn.nzz * fb
    outs = [jnp.zeros((pn.total, pn.feat), F32) for _ in range(pn.experts)]
    for k in range(nx):
        xp = x_of(nx - k)
        if k > 0:
            for i in range(nz):
                receive(act.at[xp, z_of(nz - i)], "gx", (k - 1) * nz + i, x_dev(k))
        for j in range(pn.experts):
            rows = jnp.concatenate(
                [act[xp, j * pn.nzz + zz] for zz in range(pn.nzz)], axis=1
            )
            down = dns[j, :, pl.ds(pl.multiple_of(xp * depth, depth), depth)]
            outs[j] = outs[j] + mm_nt(rows, down)

    s_row = iota((ne * 16, pn.total), 0)
    s_owner, s_tok = owner_of(iota((ne * 16, pn.total), 1))
    acc = jnp.zeros((ne * 16, pn.featp), F32)
    for j in range(pn.experts):
        put = jnp.where(s_row == s_owner * 16 + j * pn.tok + s_tok, 1.0, 0.0).astype(BF16)
        acc = acc + mm(put, pad_lanes(outs[j], pn.featp).astype(BF16))
    fs[...] = acc.astype(BF16).reshape(ne, 16, pn.featp)
    for k in far_first(ne):
        send(fs.at[e_of(k)], fr.at[me], "f", k - 1, e_dev(k))
    fr[me] = fs[me]

    ids = pad_rows(jnp.concatenate([ids_ref[r] for r in range(pn.rows)], axis=0), 8)
    coef = pad_rows(jnp.concatenate([rw_ref[r] for r in range(pn.rows)], axis=0), 8)
    c_row, c_col = iota((8, ne * 16), 0), iota((8, ne * 16), 1)
    place = c_col & 15
    expert = (c_col >> 4) * pn.experts + (place >> lt)
    used = (place < pn.experts * pn.tok) & ((place & (pn.tok - 1)) == c_row)
    mix = jnp.zeros((8, ne * 16), F32)
    for t in range(TOPK):
        mix = mix + jnp.where(used & (expert == ids[:, t : t + 1]), coef[:, t : t + 1], 0.0)
    own_row, own_col = iota((8, pn.total), 0), iota((8, pn.total), 1)
    own_at = core * (pn.total // 2) + my_y * pn.tok + own_row
    own = jnp.where((own_col == own_at) & (own_row < pn.tok), 1.0, 0.0).astype(BF16)
    own_hidden = mm(own, hidden)

    for k in range(1, ne):
        receive(fr.at[e_of(ne - k)], "f", k - 1, e_dev(k))
    returned = fr[...].reshape(ne * 16, pn.featp).astype(F32)
    mixed = own_hidden + mm(mix, returned, HIGH)
    for r in range(pn.rows):
        out_ref[r] = mixed[r * STEPS : (r + 1) * STEPS, 0 : pn.feat].astype(BF16)
    for copy in pending:
        copy.wait_send()


def on_device(
    nx,
    queries,
    new_latent,
    cache,
    lengths,
    value_up,
    out_proj,
    residual,
    norm_gain,
    route_ids,
    route_weights,
    gate_up,
    expert_down,
):
    ne = lax.axis_size("exp")
    nz = lax.axis_size("ctx") // nx
    pn = Plan(nx, nz, ne, queries, cache, out_proj, gate_up)
    keys = pn.span + LANES
    stat_lanes = nz * pn.block
    any_spec = pl.BlockSpec(memory_space=pl.ANY)
    vmem_spec = pl.BlockSpec(memory_space=pltpu.VMEM)
    fp, total = pn.featp, pn.total
    v = pltpu.VMEM
    crow = pn.rows * STEPS * pn.per
    scratch = [
        v(new_latent.shape, BF16),
        pltpu.SMEM(lengths.shape, jnp.int32),
        v(residual.shape, BF16),
        v(route_ids.shape, jnp.int32),
        v(route_weights.shape, F32),
        v((pn.rows, STEPS, pn.width, pn.heads), BF16),
        v((pn.rows, pn.width, keys), BF16),
        v(value_up.shape[1:], BF16),
        v((2, *out_proj.shape), BF16),
        v((nx, nz, pn.feat, 2 * pn.fb), BF16),
        v((pn.experts, pn.feat, pn.ffe), BF16),
        v((nx, nz, 2 * pn.vrows, fp), BF16),
        v((16, fp), BF16),
        v((ne, 16, fp), BF16),
        v((nx, pn.hl, pn.halves, crow, LATENT), BF16),
        v((nx, pn.ny, pn.halves, crow, LATENT), BF16),
        v((nx, 8, stat_lanes), F32),
        v((nx, pn.ny, 8, stat_lanes), F32),
        v((nz, pn.block, LATENT), BF16),
        v((nz - 1, pn.block, LATENT), BF16),
        v((8, stat_lanes), F32),
        v((nz - 1, 8, stat_lanes), F32),
        v((stat_lanes, LANES), F32),
        v((nx, nz, total // 2, fp), BF16),
        v((nx - 1, nz, total // 2, fp), BF16),
        v((nz, total // 2, fp), BF16),
        v((nz - 1, total // 2, fp), BF16),
        v((total // 2, fp), BF16),
        v((ne, total // 2, fp), BF16),
        v((8, LANES), F32),
        v((nx - 1, 8, LANES), F32),
        v((8, LANES), F32),
        v((nz - 1, 8, LANES), F32),
        v((nx, nz, total, 2 * pn.fb), BF16),
        v((nx - 1, nz, total, 2 * pn.fb), BF16),
        v((nz, total, 2 * pn.fb), BF16),
        v((nz - 1, total, 2 * pn.fb), BF16),
        v((nx, nz, total, pn.fb), BF16),
        v((ne, 16, fp), BF16),
        v((ne, 16, fp), BF16),
        pltpu.SemaphoreType.DMA((pn.n_remote,)),
        pltpu.SemaphoreType.DMA((pn.n_remote,)),
        pltpu.SemaphoreType.DMA((pn.n_local,)),
    ]
    return pl.pallas_call(
        functools.partial(kernel, pn),
        out_shape=jax.ShapeDtypeStruct(residual.shape, BF16),
        in_specs=[any_spec] * 7 + [vmem_spec] + [any_spec] * 4,
        out_specs=vmem_spec,
        scratch_shapes=scratch,
        compiler_params=pltpu.CompilerParams(
            collective_id=0, has_side_effects=True, vmem_limit_bytes=60 * 1024 * 1024
        ),
        name="decode_layer",
    )(
        jnp.swapaxes(queries, 2, 3),
        new_latent,
        jnp.swapaxes(cache, 1, 2),
        lengths,
        value_up,
        out_proj,
        residual,
        norm_gain,
        route_ids,
        route_weights,
        gate_up,
        jnp.swapaxes(expert_down, 1, 2),
    )


def solution(mesh, nx=CHIPS_X):
    in_specs = (
        P("exp", None, None, None),
        P("exp", None, None),
        P("exp", "ctx", None),
        P("exp"),
        P("ctx", None, None),
        P(("ctx", "exp"), None),
        P("exp", None, "ctx"),
        P("ctx"),
        P("exp", None, None),
        P("exp", None, None),
        P("exp", "ctx", None),
        P("exp", None, "ctx"),
    )
    return jax.shard_map(
        functools.partial(on_device, nx),
        mesh=mesh,
        in_specs=in_specs,
        out_specs=P("exp", None, "ctx"),
        check_vma=False,
    )
```

time: 77.1 us -> 68.1 us (0.88)
  Pallas kernels: 75.7 us -> 66.7 us
    pallas_call x1, Pallas kernels: 75.7 us -> 66.7 us  [on_device(): pl.pallas_call(functools.partial(kernel, pn), out_shape=jax.ShapeDtypeStr...]
where the time goes in v2:
time: 68.1 us; the launch traced here: 68 us
  Pallas kernels  66.7 us (98%)
  local copies, waits for them, and re-layouts  1.26 us (2%)
    pallas_call x1, Pallas kernels, on_device(): pl.pallas_call(functools.partial(kernel, pn), out_shape=jax.ShapeDtypeStr...  66.7 us

profile of v2, /device:TPU:1, one launch (start us, length us, event | category | flops | bytes accessed | tf_op | source)
XLA Modules:
  0.0 68.0 jit_solution(18076974420055884300)
XLA Ops:
  0.0 66.7 %decode_layer.1 = bf16[2,2,224]{2,1,0:T(2,128)(2,1)} custom-call(bf16[2,2,576,128]{3,2,1,0:T(8,128)(2,1)} %bitcast.5, bf16[2,2,576]{2,1,0:T(2,128)(2,1)} %nl_hbm.1, bf16[2,576,512]{2,1,0:T(8,128)(2,1)} %bitcast.4, s32[2]{0:T(128)} %len_hbm.1, bf16[4,512,128]{2,1,0:T(8,128)(2,1)} %vu_hbm.1, bf16[64,7168]{1,0:T(8,128)(2,1)} %op_hbm.1, ...), custom_call_target="tpu_custom_call" | custom-call | tf_op jit(solution)/shard_map/decode_layer/pallas_call | solution.py:696
  66.7 1.3 %copy.14 = bf16[2,2,224]{2,1,0:T(2,128)(2,1)} copy(bf16[2,2,224]{2,1,0:T(2,128)(2,1)} %decode_layer.1) | data formatting | bytes 3584

commit v3 on v2

--- a/solution.py
+++ b/solution.py
@@ -75,6 +75,7 @@
         self.zorder = far_first(nz) + [0]
         self.xorder = far_first(nx) + [0]
         self.halves = 2
+        self.parts = min(4, nz)
         self.per = nz // self.halves
         nxy = nx * self.ny - 1
         self.base, at = {}, 0
@@ -85,12 +86,12 @@
             ("a", nxy * self.halves),
             ("azs", nz - 1),
             ("az", nz - 1),
-            ("cx", (nx - 1) * self.halves),
+            ("cx", (nx - 1) * self.parts),
             ("cz", nz - 1),
             ("ce", ne - 1),
             ("sx", nx - 1),
             ("sz", nz - 1),
-            ("ex", (nx - 1) * self.halves),
+            ("ex", (nx - 1) * self.parts),
             ("ez", nz - 1),
             ("gz", nz - 1),
             ("gx", (nx - 1) * nz),
@@ -99,7 +100,7 @@
             self.base[name] = at
             at += n
         self.n_remote = at
-        self.n_local = 2 * self.rows + 10
+        self.n_local = 2 * self.rows + 12
 
 
 def joined(tops, totals):
@@ -119,7 +120,7 @@
     vu_hbm,
     op_hbm,
     res_hbm,
-    gain_ref,
+    gain_hbm,
     ids_hbm,
     rw_hbm,
     gu_hbm,
@@ -128,6 +129,7 @@
     nl_ref,
     len_ref,
     res_ref,
+    gain_ref,
     ids_ref,
     rw_ref,
     qs,
@@ -204,6 +206,27 @@
 
     core_dev = (ctx, me + 1 - 2 * core)
 
+    local_at = [0]
+
+    def local(src, dst):
+        copy = pltpu.make_async_copy(src, dst, local_sems.at[local_at[0]])
+        local_at[0] += 1
+        copy.start()
+        return copy
+
+    q_copies, k_copies = [], []
+    for r in range(pn.rows):
+        q_copies.append(local(q_hbm.at[r], qs.at[r]))
+        k_copies.append(local(cache_hbm.at[r], ks.at[r, :, pl.ds(0, pn.span)]))
+    small_copies = [
+        local(nl_hbm, nl_ref),
+        local(len_hbm, len_ref),
+        local(res_hbm, res_ref),
+        local(ids_hbm, ids_ref),
+        local(rw_hbm, rw_ref),
+        local(gain_hbm, gain_ref),
+    ]
+
     xy_far = [
         (kx, ky) for kx in far_first(nx) + [0] for ky in far_first(ny) + [0] if kx or ky
     ]
@@ -234,28 +257,6 @@
 
     def receive(dst, name, slot, dev):
         remote(dst, dst, name, slot, dev).wait_recv()
-
-    local_at = [0]
-
-    def local(src, dst):
-        copy = pltpu.make_async_copy(src, dst, local_sems.at[local_at[0]])
-        local_at[0] += 1
-        copy.start()
-        return copy
-
-    q_copies = [local(q_hbm.at[r], qs.at[r]) for r in range(pn.rows)]
-    k_copies = [
-        local(cache_hbm.at[r], ks.at[r, :, pl.ds(0, pn.span)]) for r in range(pn.rows)
-    ]
-    small_copies = [
-        local(nl_hbm, nl_ref),
-        local(len_hbm, len_ref),
-        local(res_hbm, res_ref),
-        local(ids_hbm, ids_ref),
-        local(rw_hbm, rw_ref),
-    ]
-    op_copy = local(op_hbm, ops.at[core])
-    vu_copy = local(vu_hbm.at[my_y], vus)
 
     qrows = STEPS * pn.heads
     keys = pn.span + LANES
@@ -286,23 +287,10 @@
     rb[...] = pad_rows(pad_lanes(res_rows, pn.featp), 16).astype(BF16)
     ra[me] = rb[...]
 
-    gu_sem, dn_copy = local_sems.at[pn.n_local - 1], None
     partial, peaks, denoms = [], [], []
     for r in range(pn.rows):
         q_copies[r].wait()
         k_copies[r].wait()
-        if r == pn.rows - 1:
-            for x in range(nx):
-                for z in range(nz):
-                    j, zz = z // pn.nzz, z % pn.nzz
-                    for g in range(2):
-                        at = g * pn.ffe + (x * pn.nzz + zz) * pn.fb
-                        pltpu.make_async_copy(
-                            gu_hbm.at[j, :, pl.ds(at, pn.fb)],
-                            gus.at[x, z, :, pl.ds(g * pn.fb, pn.fb)],
-                            gu_sem,
-                        ).start()
-            dn_copy = local(dn_hbm, dns)
         qp = functools.reduce(
             jnp.add,
             [
@@ -324,6 +312,24 @@
 
     span_rows = STEPS * per
     groups = nx * pn.hl * halves
+    crow = pn.rows * span_rows
+    merged = jnp.concatenate(
+        [p.reshape(groups, span_rows, LATENT) for p in partial], axis=1
+    )
+    os_[...] = merged.astype(BF16).reshape(nx, pn.hl, halves, crow, LATENT)
+
+    def send_partial(h):
+        for kx, ky in xy_far:
+            send(
+                os_.at[x_of(kx), y_of(ky), h],
+                oxr.at[kx, my_y, h],
+                "a",
+                (kx * ny + ky - 1) * halves + h,
+                xy_dev(kx, ky),
+            )
+
+    pl.semaphore_wait(barrier, len(peers))
+    send_partial(0)
     lane = iota((qrows, LANES), 1)
     stat = [
         jnp.where(lane == 0, p, jnp.where(lane == 1, d, 0.0)) for p, d in zip(peaks, denoms)
@@ -331,29 +337,28 @@
     stat = jnp.concatenate([s.reshape(groups, span_rows, LANES) for s in stat], axis=1)
     stat = stat.reshape(nx, nz * pn.block, LANES)
     for x in range(nx):
-        sxs[x] = jnp.transpose(stat[x])[0:8, :]
-    sxr[0, my_y] = sxs[my_x]
-    crow = pn.rows * span_rows
-    merged = jnp.concatenate(
-        [p.reshape(groups, span_rows, LATENT) for p in partial], axis=1
-    )
-    os_[...] = merged.astype(BF16).reshape(nx, pn.hl, halves, crow, LATENT)
-    oxr[0, my_y] = os_[my_x, my_y]
-
-    pl.semaphore_wait(barrier, len(peers))
+        sxs[x] = jnp.transpose(stat[x])[0:2, :]
     for kx, ky in xy_far:
         slot = kx * ny + ky - 1
         send(sxs.at[x_of(kx)], sxr.at[kx, my_y], "as", slot, xy_dev(kx, ky))
-    for h in range(halves):
-        for kx, ky in xy_far:
-            slot = (kx * ny + ky - 1) * halves + h
-            send(
-                os_.at[x_of(kx), y_of(ky), h],
-                oxr.at[kx, my_y, h],
-                "a",
-                slot,
-                xy_dev(kx, ky),
-            )
+    for h in range(1, halves):
+        send_partial(h)
+    sxr[0, my_y] = sxs[my_x]
+    oxr[0, my_y] = os_[my_x, my_y]
+    op_copy = local(op_hbm, ops.at[core])
+    vu_copy = local(vu_hbm.at[my_y], vus)
+    gu_sem = local_sems.at[pn.n_local - 1]
+    for x in range(nx):
+        for z in range(nz):
+            j, zz = z // pn.nzz, z % pn.nzz
+            for g in range(2):
+                at = g * pn.ffe + (x * pn.nzz + zz) * pn.fb
+                pltpu.make_async_copy(
+                    gu_hbm.at[j, :, pl.ds(at, pn.fb)],
+                    gus.at[x, z, :, pl.ds(g * pn.fb, pn.fb)],
+                    gu_sem,
+                ).start()
+    dn_copy = local(dn_hbm, dns)
     op_copy.wait()
     send(ops.at[core], ops.at[core], "op", 0, core_dev)
     for k in range(1, ne):
@@ -394,7 +399,7 @@
             for y in range(ny)
         ]
         stat.append(mm(turn, jnp.concatenate(rows, axis=0), HIGH))
-    szs[...] = jnp.transpose(jnp.concatenate(stat, axis=0))[0:8, :]
+    szs[...] = jnp.transpose(jnp.concatenate(stat, axis=0))[0:2, :]
     for k in far_first(nz):
         send(szs, szr.at[k - 1], "azs", k - 1, z_dev(k))
     turn = turn.astype(BF16)
@@ -457,13 +462,15 @@
         acc = acc + cols[:, k : k + 1] * ozr[k - 1].astype(F32)
     values = mm(acc.astype(BF16), vus[...]).astype(BF16)
 
+    each = nz // pn.parts
+
     def partner_chunk(h):
-        return pl.ds(h * per, per)
-
-    for h in range(halves):
+        return pl.ds(h * each, each)
+
+    for h in range(pn.parts):
         for k in xorder:
-            for p in range(per):
-                place = h * per + p
+            for p in range(each):
+                place = h * each + p
                 block = mm(values, opw[x_of(k), z_of(zorder[place])])
                 cs[k, place] = block.astype(BF16)
             if k > 0:
@@ -471,16 +478,16 @@
                     cs.at[k, partner_chunk(h)],
                     cr.at[k - 1, partner_chunk(h)],
                     "cx",
-                    (k - 1) * halves + h,
+                    (k - 1) * pn.parts + h,
                     x_dev(k),
                 )
-    for h in range(halves):
+    for h in range(pn.parts):
         for k in range(1, nx):
             receive(
-                cr.at[k - 1, partner_chunk(h)], "cx", (k - 1) * halves + h, x_dev(k)
+                cr.at[k - 1, partner_chunk(h)], "cx", (k - 1) * pn.parts + h, x_dev(k)
             )
-        for p in range(per):
-            place = h * per + p
+        for p in range(each):
+            place = h * each + p
             acc = cs[0, place].astype(F32)
             for i in range(1, nx):
                 acc = acc + cr[i - 1, place].astype(F32)
@@ -510,10 +517,10 @@
     scaled = (hidden_f[:, 0 : pn.feat] * gain_ref[...].reshape(1, pn.feat)).astype(BF16)
     pltpu.make_async_copy(gus, gus, gu_sem).wait()
     fb = pn.fb
-    for h in range(halves):
+    for h in range(pn.parts):
         for k in xorder:
-            for p in range(per):
-                place = h * per + p
+            for p in range(each):
+                place = h * each + p
                 block = mm(scaled, gus[x_of(k), z_of(zorder[place])])
                 es[k, place] = block.astype(BF16)
             if k > 0:
@@ -521,13 +528,13 @@
                     es.at[k, partner_chunk(h)],
                     exr.at[k - 1, partner_chunk(h)],
                     "ex",
-                    (k - 1) * halves + h,
+                    (k - 1) * pn.parts + h,
                     x_dev(k),
                 )
         if h == 0:
             squares = jnp.sum(hidden_f * hidden_f, axis=1, keepdims=True)
             squares = pad_rows(jnp.broadcast_to(squares, (pn.total, LANES)), LANES)
-            qxs[...] = jnp.transpose(squares)[0:8, :]
+            qxs[...] = jnp.transpose(squares)[0:2, :]
             for k in far_first(nx):
                 send(qxs, qxr.at[k - 1], "sx", k - 1, x_dev(k))
     acc = qxs[...]
@@ -535,13 +542,13 @@
         receive(qxr.at[k - 1], "sx", k - 1, x_dev(k))
         acc = acc + qxr[k - 1]
     qzs[...] = acc
-    for h in range(halves):
+    for h in range(pn.parts):
         for k in range(1, nx):
             receive(
-                exr.at[k - 1, partner_chunk(h)], "ex", (k - 1) * halves + h, x_dev(k)
+                exr.at[k - 1, partner_chunk(h)], "ex", (k - 1) * pn.parts + h, x_dev(k)
             )
-        for p in range(per):
-            place = h * per + p
+        for p in range(each):
+            place = h * each + p
             acc = es[0, place].astype(F32)
             for i in range(1, nx):
                 acc = acc + exr[i - 1, place].astype(F32)
@@ -576,7 +583,7 @@
             send(block, block, "gx", (i - 1) * nz + k, x_dev(i))
     depth = pn.nzz * fb
     outs = [jnp.zeros((pn.total, pn.feat), F32) for _ in range(pn.experts)]
-    for k in range(nx):
+    for k in [0] + list(reversed(far_first(nx))):
         xp = x_of(nx - k)
         if k > 0:
             for i in range(nz):
@@ -613,13 +620,15 @@
     own = jnp.where((own_col == own_at) & (own_row < pn.tok), 1.0, 0.0).astype(BF16)
     own_hidden = mm(own, hidden)
 
+    for copy in pending[: 1 - ne]:
+        copy.wait_send()
     for k in range(1, ne):
         receive(fr.at[e_of(ne - k)], "f", k - 1, e_dev(k))
     returned = fr[...].reshape(ne * 16, pn.featp).astype(F32)
     mixed = own_hidden + mm(mix, returned, HIGH)
     for r in range(pn.rows):
         out_ref[r] = mixed[r * STEPS : (r + 1) * STEPS, 0 : pn.feat].astype(BF16)
-    for copy in pending:
+    for copy in pending[1 - ne :]:
         copy.wait_send()
 
 
@@ -652,6 +661,7 @@
         v(new_latent.shape, BF16),
         pltpu.SMEM(lengths.shape, jnp.int32),
         v(residual.shape, BF16),
+        v(norm_gain.shape, F32),
         v(route_ids.shape, jnp.int32),
         v(route_weights.shape, F32),
         v((pn.rows, STEPS, pn.width, pn.heads), BF16),
@@ -665,12 +675,12 @@
         v((ne, 16, fp), BF16),
         v((nx, pn.hl, pn.halves, crow, LATENT), BF16),
         v((nx, pn.ny, pn.halves, crow, LATENT), BF16),
-        v((nx, 8, stat_lanes), F32),
-        v((nx, pn.ny, 8, stat_lanes), F32),
+        v((nx, 2, stat_lanes), F32),
+        v((nx, pn.ny, 2, stat_lanes), F32),
         v((nz, pn.block, LATENT), BF16),
         v((nz - 1, pn.block, LATENT), BF16),
-        v((8, stat_lanes), F32),
-        v((nz - 1, 8, stat_lanes), F32),
+        v((2, stat_lanes), F32),
+        v((nz - 1, 2, stat_lanes), F32),
         v((stat_lanes, LANES), F32),
         v((nx, nz, total // 2, fp), BF16),
         v((nx - 1, nz, total // 2, fp), BF16),
@@ -678,10 +688,10 @@
         v((nz - 1, total // 2, fp), BF16),
         v((total // 2, fp), BF16),
         v((ne, total // 2, fp), BF16),
-        v((8, LANES), F32),
-        v((nx - 1, 8, LANES), F32),
-        v((8, LANES), F32),
-        v((nz - 1, 8, LANES), F32),
+        v((2, LANES), F32),
+        v((nx - 1, 2, LANES), F32),
+        v((2, LANES), F32),
+        v((nz - 1, 2, LANES), F32),
         v((nx, nz, total, 2 * pn.fb), BF16),
         v((nx - 1, nz, total, 2 * pn.fb), BF16),
         v((nz, total, 2 * pn.fb), BF16),
@@ -696,7 +706,7 @@
     return pl.pallas_call(
         functools.partial(kernel, pn),
         out_shape=jax.ShapeDtypeStruct(residual.shape, BF16),
-        in_specs=[any_spec] * 7 + [vmem_spec] + [any_spec] * 4,
+        in_specs=[any_spec] * 12,
         out_specs=vmem_spec,
         scratch_shapes=scratch,
         compiler_params=pltpu.CompilerParams(

time: 68.1 us -> 65.8 us (0.966)
  Pallas kernels: 66.7 us -> 64.4 us
    pallas_call x1, Pallas kernels: 66.7 us -> 64.4 us  [on_device(): pl.pallas_call(functools.partial(kernel, pn), out_shape=jax.ShapeDtypeStr...]
where the time goes in v3:
time: 65.8 us; the launch traced here: 65.7 us
  Pallas kernels  64.4 us (98%)
  local copies, waits for them, and re-layouts  1.26 us (2%)
    pallas_call x1, Pallas kernels, on_device(): pl.pallas_call(functools.partial(kernel, pn), out_shape=jax.ShapeDtypeStr...  64.4 us

profile of v3, /device:TPU:1, one launch (start us, length us, event | category | flops | bytes accessed | tf_op | source)
XLA Modules:
  0.0 65.7 jit_solution(892078340641898147)
XLA Ops:
  0.0 64.4 %decode_layer.1 = bf16[2,2,224]{2,1,0:T(2,128)(2,1)} custom-call(bf16[2,2,576,128]{3,2,1,0:T(8,128)(2,1)} %bitcast.5, bf16[2,2,576]{2,1,0:T(2,128)(2,1)} %nl_hbm.1, bf16[2,576,512]{2,1,0:T(8,128)(2,1)} %bitcast.4, s32[2]{0:T(128)} %len_hbm.1, bf16[4,512,128]{2,1,0:T(8,128)(2,1)} %vu_hbm.1, bf16[64,7168]{1,0:T(8,128)(2,1)} %op_hbm.1, ...), custom_call_target="tpu_custom_call" | custom-call | tf_op jit(solution)/shard_map/decode_layer/pallas_call | solution.py:706
  64.5 1.3 %copy.14 = bf16[2,2,224]{2,1,0:T(2,128)(2,1)} copy(bf16[2,2,224]{2,1,0:T(2,128)(2,1)} %decode_layer.1) | data formatting | bytes 3584

commit v4 on v3

--- a/solution.py
+++ b/solution.py
@@ -231,11 +231,13 @@
         (kx, ky) for kx in far_first(nx) + [0] for ky in far_first(ny) + [0] if kx or ky
     ]
     barrier = pltpu.get_barrier_semaphore()
-    peers = (
-        [z_dev(k) for k in far_first(nz)]
-        + [xy_dev(kx, ky) for kx, ky in xy_far]
-        + [(ctx, 2 * y_of(ky) + 1 - core) for ky in range(ny)]
-    )
+    def hops(k, n):
+        return min(k, n - k)
+
+    reached = [(hops(k, nz), z_dev(k)) for k in far_first(nz)]
+    reached += [(hops(kx, nx) + hops(ky, ny), xy_dev(kx, ky)) for kx, ky in xy_far]
+    reached += [(hops(ky, ny), (ctx, 2 * y_of(ky) + 1 - core)) for ky in range(ny)]
+    peers = [dev for _, dev in sorted(reached, key=lambda item: -item[0])]
     for dev in peers:
         pl.semaphore_signal(barrier, inc=1, device_id=dev, device_id_type=MESH)
 
@@ -287,28 +289,37 @@
     rb[...] = pad_rows(pad_lanes(res_rows, pn.featp), 16).astype(BF16)
     ra[me] = rb[...]
 
-    partial, peaks, denoms = [], [], []
-    for r in range(pn.rows):
-        q_copies[r].wait()
-        k_copies[r].wait()
-        qp = functools.reduce(
+    for copy in q_copies + k_copies:
+        copy.wait()
+    every = range(pn.rows)
+    turned = [
+        functools.reduce(
             jnp.add,
             [
                 mm_nt(perm[:, s * pn.heads : (s + 1) * pn.heads], qs[r, s])
                 for s in range(STEPS)
             ],
         ).astype(BF16)
-        scores = mm(qp, ks[r])
-        visible = ((col < pn.span) & (position < len_ref[r])) | is_fresh
-        scores = jnp.where(visible, scores * qk_scale, -1e30)
-        peak = jnp.max(scores, axis=1, keepdims=True)
-        weights = jnp.where(visible, jnp.exp(scores - peak), 0.0)
-        denom = jnp.sum(weights, axis=1, keepdims=True)
-        mixture = mm_nt(weights.astype(BF16), ks[r, pl.ds(0, LATENT), :])
-        inv = jnp.where(denom > 0.0, 1.0 / jnp.where(denom > 0.0, denom, 1.0), 0.0)
-        partial.append(mixture * inv)
-        peaks.append(peak)
-        denoms.append(denom)
+        for r in every
+    ]
+    scores = [mm(turned[r], ks[r]) for r in every]
+    visible = [
+        ((col < pn.span) & (position < len_ref[r])) | is_fresh for r in every
+    ]
+    scores = [jnp.where(visible[r], scores[r] * qk_scale, -1e30) for r in every]
+    peaks = [jnp.max(s, axis=1, keepdims=True) for s in scores]
+    weights = [
+        jnp.where(visible[r], jnp.exp(scores[r] - peaks[r]), 0.0) for r in every
+    ]
+    denoms = [jnp.sum(w, axis=1, keepdims=True) for w in weights]
+    mixtures = [
+        mm_nt(weights[r].astype(BF16), ks[r, pl.ds(0, LATENT), :]) for r in every
+    ]
+    partial = [
+        mixtures[r]
+        * jnp.where(denoms[r] > 0.0, 1.0 / jnp.where(denoms[r] > 0.0, denoms[r], 1.0), 0.0)
+        for r in every
+    ]
 
     span_rows = STEPS * per
     groups = nx * pn.hl * halves

time: 65.8 us -> 65.1 us (0.989)
  Pallas kernels: 64.4 us -> 63.7 us
    pallas_call x1, Pallas kernels: 64.4 us -> 63.7 us  [on_device(): pl.pallas_call(functools.partial(kernel, pn), out_shape=jax.ShapeDtypeStr...]
where the time goes in v4:
time: 65.1 us; the launch traced here: 65 us
  Pallas kernels  63.7 us (98%)
  local copies, waits for them, and re-layouts  1.26 us (2%)
    pallas_call x1, Pallas kernels, on_device(): pl.pallas_call(functools.partial(kernel, pn), out_shape=jax.ShapeDtypeStr...  63.7 us

profile of v4, /device:TPU:1, one launch (start us, length us, event | category | flops | bytes accessed | tf_op | source)
XLA Modules:
  0.0 65.0 jit_solution(15491411814435632355)
XLA Ops:
  0.0 63.7 %decode_layer.1 = bf16[2,2,224]{2,1,0:T(2,128)(2,1)} custom-call(bf16[2,2,576,128]{3,2,1,0:T(8,128)(2,1)} %bitcast.5, bf16[2,2,576]{2,1,0:T(2,128)(2,1)} %nl_hbm.1, bf16[2,576,512]{2,1,0:T(8,128)(2,1)} %bitcast.4, s32[2]{0:T(128)} %len_hbm.1, bf16[4,512,128]{2,1,0:T(8,128)(2,1)} %vu_hbm.1, bf16[64,7168]{1,0:T(8,128)(2,1)} %op_hbm.1, ...), custom_call_target="tpu_custom_call" | custom-call | tf_op jit(solution)/shard_map/decode_layer/pallas_call | solution.py:717
  63.7 1.3 %copy.14 = bf16[2,2,224]{2,1,0:T(2,128)(2,1)} copy(bf16[2,2,224]{2,1,0:T(2,128)(2,1)} %decode_layer.1) | data formatting | bytes 3584

commit v5 on v4

--- a/solution.py
+++ b/solution.py
@@ -339,8 +339,6 @@
                 xy_dev(kx, ky),
             )
 
-    pl.semaphore_wait(barrier, len(peers))
-    send_partial(0)
     lane = iota((qrows, LANES), 1)
     stat = [
         jnp.where(lane == 0, p, jnp.where(lane == 1, d, 0.0)) for p, d in zip(peaks, denoms)
@@ -349,9 +347,11 @@
     stat = stat.reshape(nx, nz * pn.block, LANES)
     for x in range(nx):
         sxs[x] = jnp.transpose(stat[x])[0:2, :]
+    pl.semaphore_wait(barrier, len(peers))
     for kx, ky in xy_far:
         slot = kx * ny + ky - 1
         send(sxs.at[x_of(kx)], sxr.at[kx, my_y], "as", slot, xy_dev(kx, ky))
+    send_partial(0)
     for h in range(1, halves):
         send_partial(h)
     sxr[0, my_y] = sxs[my_x]

time: 65.1 us -> 64.6 us (level)
  no operation moved by 1% of the time
where the time goes in v5:
time: 64.6 us; the launch traced here: 64.5 us
  Pallas kernels  63.2 us (98%)
  local copies, waits for them, and re-layouts  1.26 us (2%)
    pallas_call x1, Pallas kernels, on_device(): pl.pallas_call(functools.partial(kernel, pn), out_shape=jax.ShapeDtypeStr...  63.2 us

profile of v5, /device:TPU:1, one launch (start us, length us, event | category | flops | bytes accessed | tf_op | source)
XLA Modules:
  0.0 64.5 jit_solution(9867421034973271912)
XLA Ops:
  0.0 63.2 %decode_layer.1 = bf16[2,2,224]{2,1,0:T(2,128)(2,1)} custom-call(bf16[2,2,576,128]{3,2,1,0:T(8,128)(2,1)} %bitcast.5, bf16[2,2,576]{2,1,0:T(2,128)(2,1)} %nl_hbm.1, bf16[2,576,512]{2,1,0:T(8,128)(2,1)} %bitcast.4, s32[2]{0:T(128)} %len_hbm.1, bf16[4,512,128]{2,1,0:T(8,128)(2,1)} %vu_hbm.1, bf16[64,7168]{1,0:T(8,128)(2,1)} %op_hbm.1, ...), custom_call_target="tpu_custom_call" | custom-call | tf_op jit(solution)/shard_map/decode_layer/pallas_call | solution.py:717
  63.2 1.3 %copy.14 = bf16[2,2,224]{2,1,0:T(2,128)(2,1)} copy(bf16[2,2,224]{2,1,0:T(2,128)(2,1)} %decode_layer.1) | data formatting | bytes 3584
